TPU v7x, 256 devices: a whole 4x4x8 slice. The times are simulated.
256 devices in a mesh: azim: 32 (over z, y_lo, core), radax: 8 (over y_hi, x).
Axes of the slice: x: 4, y: 4 (y_hi: 2, y_lo: 2; y = y_hi * 2 + y_lo), z: 8, core: 2. Of those that a mesh axis runs over, the one named last changes fastest.
Arguments:
- solution: float32 [256, 64, 16, 320], P('azim', 'radax'), may hold values from -6 to 6
- metric: float32 [256, 64, 16, 3], P('azim', 'radax'), may hold values from 1 to 4
- intersections: int32 [32, 2, 3, 8], P('azim'), may hold values from 0 to 15, as said below
- counts: int32 [32, 2], P('azim'), may hold values from 4 to 8, as said below
- projections: float32 [4, 16, 4, 4], replicated, may hold values from -3 to 3
Outputs:
- advanced: float32 [256, 64, 16, 320], P('azim', 'radax')
Inputs may be any that keep to these rules, and one draw needn't show every extreme that they name: intersections[s, b] holds 8 slots of (rotor face's azimuthal index within sector (s - 1 + b) mod 32, stator face's azimuthal index within sector s, segment kind); face indices are below 8, kinds below 16; slots at or after counts[s, b] are padding. `counts`: used slots of each list; some sector fills its first list, some sector its second.
All inputs are finite; a program needn't handle non-finite values.
Results may differ from a plain program's by a relative error of at most 0.0001.
Values sent between devices are 32-bit elements; how exact they have to be, the bound alone decides.
No kernel may reach another device: no remote copies, remote signals or barrier semaphores. Data moves between devices by JAX's collectives and lax.ppermute only.
A program may use at most 128 MiB of HBM per device.

v0:
```python
import functools
import jax
import jax.numpy as jnp
import numpy as np
from jax import lax
from jax.experimental import pallas as pl
from jax.experimental.pallas import tpu as pltpu
from jax.sharding import PartitionSpec as P

time_step = 0.02
mean_flow = (0.5, 0.0, 0.4)
speeds = tuple(abs(u) + 1.0 for u in mean_flow)
highest = lax.Precision.HIGHEST
f32 = jnp.float32


def line_numbers():
    points = np.array([-1.0, -1.0 / np.sqrt(5.0), 1.0 / np.sqrt(5.0), 1.0])
    barycentric = np.array(
        [1.0 / np.prod([points[j] - points[k] for k in range(4) if k != j]) for j in range(4)]
    )
    single = np.zeros((4, 4))
    for i in range(4):
        for j in range(4):
            if i != j:
                single[i, j] = barycentric[j] / barycentric[i] / (points[i] - points[j])
        single[i, i] = -np.sum(single[i])
    return single


D = line_numbers()


def row(f, i, j, k):
    return (f * 64 + 16 * i + 4 * j + k) * 8


def tile(ref, f, i, j, k):
    return ref[pl.ds(row(f, i, j, k), 8), :]


def lane_ids():
    return lax.broadcasted_iota(jnp.int32, (8, 128), 1)


def minus_slope(x, scale):
    e0, e1 = x[0] - x[3], x[1] - x[2]
    t = (x[0] + x[3]) - (x[1] + x[2])
    c = -scale * 0.5
    outer = (c * (D[0, 0] - D[0, 3])) * e0 + (c * (D[0, 1] - D[0, 2])) * e1
    inner = (c * (D[1, 0] - D[1, 3])) * e0 + (c * (D[1, 1] - D[1, 2])) * e1
    outer_t = (c * (D[0, 0] + D[0, 3])) * t
    inner_t = (c * (D[1, 0] + D[1, 3])) * t
    return [outer + outer_t, inner + inner_t, inner - inner_t, outer - outer_t]


def line_terms(d, x, low, high):
    flow, speed = mean_flow[d], speeds[d]
    w0 = [3.0 * v for v in low]
    w3 = [3.0 * v for v in high]
    mine = 1 + d
    slopes = {}
    for f in (mine, 4):
        h = minus_slope(x[f], 1.0)
        h[0] = h[0] + w0[f]
        h[3] = h[3] - w3[f]
        slopes[f] = h
    result = []
    for f in range(5):
        if f == mine:
            r = [slopes[4][i] + flow * slopes[mine][i] if flow else slopes[4][i] for i in range(4)]
            r[0] = r[0] + speed * w0[f]
            r[3] = r[3] + speed * w3[f]
        elif f == 4:
            r = [slopes[mine][i] + flow * slopes[4][i] if flow else slopes[mine][i] for i in range(4)]
            r[0] = r[0] + speed * w0[f]
            r[3] = r[3] + speed * w3[f]
        else:
            r = minus_slope(x[f], flow) if flow else [None] * 4
            if f == 0:
                r = [slopes[mine][i] if r[i] is None else r[i] + slopes[mine][i] for i in range(4)]
            lows, highs = (speed + flow) * w0[f], (speed - flow) * w3[f]
            r[0] = lows if r[0] is None else r[0] + lows
            r[3] = highs if r[3] is None else r[3] + highs
        result.append(r)
    return result


def apply_operator(q, m, acc, az, rad, mortar, first, write):
    lanes = lane_ids()
    axial = lanes & 15
    scale = m[pl.ds(16, 8), :]
    for i in range(4):
        for j in range(4):
            x = [[tile(q, f, i, j, k) for k in range(4)] for f in range(5)]
            low, high = [], []
            for f in range(5):
                before = jnp.where(axial == 0, 0.0, pltpu.roll(x[f][3], 1, 1))
                after = jnp.where(axial == 15, 0.0, pltpu.roll(x[f][0], 127, 1))
                to_stator, to_rotor = mortar(f, i, j)
                low.append(jnp.where(axial == 8, to_stator, before - x[f][0]))
                high.append(jnp.where(axial == 7, to_rotor, after - x[f][3]))
            terms = line_terms(2, x, low, high)
            for f in range(5):
                for k in range(4):
                    acc[pl.ds(row(f, i, j, k), 8), :] = first(x[f][k], f, i, j, k) + scale * terms[f][k]
    scale = m[pl.ds(0, 8), :]
    for j in range(4):
        for k in range(4):
            x = [[tile(q, f, i, j, k) for i in range(4)] for f in range(5)]
            low, high = [], []
            for f in range(5):
                before, after = az(f, j, k, x[f][0], x[f][3])
                low.append(before - x[f][0])
                high.append(after - x[f][3])
            terms = line_terms(0, x, low, high)
            for f in range(5):
                for i in range(4):
                    if terms[f][i] is not None:
                        at = pl.ds(row(f, i, j, k), 8)
                        acc[at, :] = acc[at, :] + scale * terms[f][i]
    scale = m[pl.ds(8, 8), :]
    for i in range(4):
        for k in range(4):
            x = [[tile(q, f, i, j, k) for j in range(4)] for f in range(5)]
            low, high = [], []
            for f in range(5):
                before, after = rad(f, i, k, x[f][0], x[f][3])
                low.append(before - x[f][0])
                high.append(after - x[f][3])
            terms = line_terms(1, x, low, high)
            for f in range(5):
                for j in range(4):
                    if terms[f][j] is not None:
                        at = pl.ds(row(f, i, j, k), 8)
                        write(f, i, j, k, acc[at, :] + scale * terms[f][j])
                    else:
                        write(f, i, j, k, None)


def pack_faces(q, par, own, az0, az1, r0, r1, lists):
    lanes = lane_ids()
    even = par[0] == 0
    for f in range(5):
        at = pl.ds(f * 16, 16)
        high = q[pl.ds((f * 64 + 48) * 8 + 7, 16, stride=8), :]
        low = q[pl.ds(f * 64 * 8, 16, stride=8), :]
        az0[at, :] = jnp.where(even, high, low)
        az1[at, :] = jnp.where(even, low, high)
    spot = lanes & 15
    for i in range(4):
        for block, fields in ((0, range(4)), (1, (4,))):
            rotor = jnp.zeros((8, 128), f32)
            stator = jnp.zeros((8, 128), f32)
            for f in fields:
                for j in range(4):
                    p = 4 * (f % 4) + j
                    rotor = jnp.where(spot == p, pltpu.roll(tile(q, f, i, j, 3), (p - 7) % 128, 1), rotor)
                    stator = jnp.where(spot == p, pltpu.roll(tile(q, f, i, j, 0), (p - 8) % 128, 1), stator)
            at = pl.ds(80 + block * 32 + i * 8, 8)
            az0[at, :] = jnp.where(even, rotor, stator)
            az1[at, :] = jnp.where(even, stator, rotor)
            own[pl.ds(block * 32 + i * 8, 8), :] = rotor
            own[pl.ds(64 + block * 32 + i * 8, 8), :] = stator
    if lists is not None:
        az0[pl.ds(144, 8), :] = lists[pl.ds(0, 8), :]
        az1[pl.ds(144, 8), :] = lists[pl.ds(0, 8), :]
    outward = par[1] == 0
    place = lanes >> 4
    for g in range(10):
        high = jnp.zeros((8, 128), f32)
        low = jnp.zeros((8, 128), f32)
        for p in range(8):
            f, n = divmod(g * 8 + p, 16)
            i, k = divmod(n, 4)
            high = jnp.where(place == p, pltpu.roll(tile(q, f, i, 3, k), (16 * (p - 7)) % 128, 1), high)
            low = jnp.where(place == p, pltpu.roll(tile(q, f, i, 0, k), (16 * p) % 128, 1), low)
        at = pl.ds(g * 8, 8)
        r0[at, :] = jnp.where(outward, high, low)
        r1[at, :] = jnp.where(outward, low, high)


def outsides(par, ga0, ga1, gr0, gr1):
    even = par[0] == 0
    outward = par[1] == 0
    sub = lax.broadcasted_iota(jnp.int32, (8, 128), 0)
    lanes = lane_ids()
    first, last = par[2] == 0, par[2] == 7

    def az(f, j, k, low_inside, high_inside):
        at = pl.ds(f * 16 + 4 * j + k, 1)
        one, two = ga0[at, :], ga1[at, :]
        before = jnp.where(even, two, one)
        after = jnp.where(even, one, two)
        return (
            jnp.where(sub == 0, before, pltpu.roll(high_inside, 1, 0)),
            jnp.where(sub == 7, after, pltpu.roll(low_inside, 7, 0)),
        )

    def rad(f, i, k, low_inside, high_inside):
        g, p = divmod(f * 16 + 4 * i + k, 8)
        at = pl.ds(g * 8, 8)
        one, two = gr0[at, :], gr1[at, :]
        before = jnp.where(first, 0.0, jnp.where(outward, two, one))
        after = jnp.where(last, 0.0, jnp.where(outward, one, two))
        high = jnp.where(lanes >= 112, pltpu.roll(before, (112 - 16 * p) % 128, 1), high_inside)
        low = jnp.where(lanes < 16, pltpu.roll(after, (128 - 16 * p) % 128, 1), low_inside)
        return pltpu.roll(high, 16, 1), pltpu.roll(low, 112, 1)

    return az, rad


def mortar_matrix(lists, following, tables):
    slots = jnp.concatenate([lists, following], axis=0)
    rotor, stator, kind, used = (slots[:, c : c + 1] for c in range(4))
    lanes = lax.broadcasted_iota(jnp.int32, (24, 128), 1)
    pick = (lanes.astype(f32) == kind).astype(f32)
    face = (lanes & 7).astype(f32)
    on_rotor = (face == rotor).astype(f32)
    on_stator = (face == stator).astype(f32) * 1.0
    entries = jnp.dot(pick, tables, precision=highest, preferred_element_type=f32)
    order = lax.broadcasted_iota(jnp.int32, (24, 128), 0)
    p_rot = entries[:, 0:128] * on_rotor
    p_sta = -entries[:, 128:256] * on_stator
    q_rot = -entries[:, 256:384] * on_rotor * used
    q_sta = entries[:, 384:512] * on_stator * used
    first = (order < 8).astype(f32)
    third = (order >= 16).astype(f32)
    b_parts = [p_rot * first, p_rot * (1.0 - first), p_sta * (1.0 - third), p_sta * third]
    c_parts = [q_sta * (1.0 - third), q_rot * (1.0 - first)]
    b_all = jnp.concatenate(
        [jnp.concatenate([b[:, 32 * m : 32 * m + 32] for b in b_parts], axis=1) for m in range(4)], axis=0
    )
    c_all = jnp.concatenate(
        [jnp.concatenate([c[:, 32 * m : 32 * m + 32] for c in c_parts], axis=1) for m in range(4)], axis=0
    )
    return lax.dot_general(
        c_all, b_all, (((0,), (0,)), ((), ())), precision=highest, preferred_element_type=f32
    )


def mortar_terms(par, matrix, own, ga0, ga1, placed):
    even = par[0] == 0
    blocks = []
    for block in range(2):
        at = pl.ds(80 + block * 32, 32)
        one, two = ga0[at, :], ga1[at, :]
        blocks.append(
            jnp.concatenate(
                [
                    jnp.where(even, two, one),
                    own[pl.ds(block * 32, 32), :],
                    own[pl.ds(64 + block * 32, 32), :],
                    jnp.where(even, one, two),
                ],
                axis=0,
            )
        )
    traces = jnp.concatenate(blocks, axis=1)
    placed[...] = jnp.dot(matrix, traces, precision=highest, preferred_element_type=f32)

    def mortar(f, i, j):
        block, p = divmod(4 * f + j, 16)
        at = pl.ds(128 * block, 128)
        to_stator = pltpu.roll(placed[pl.ds(8 * i, 8), at], (8 - p) % 128, 1)
        to_rotor = pltpu.roll(placed[pl.ds(32 + 8 * i, 8), at], (7 - p) % 128, 1)
        return to_stator, to_rotor

    return mortar


def enter_kernel(par, nat, metric, lists, q, m, own, az0, az1, r0, r1):
    for a in range(8):
        for c in (0, 128, 256):
            width = min(128, 320 - c)
            q[pl.ds(c * 8 + a, width, stride=8), :] = nat[a, :, c : c + width].T
        scaled = time_step * metric[a].T
        for d in range(3):
            m[pl.ds(d * 8 + a, 1), :] = scaled[d : d + 1]
    pack_faces(q, par, own, az0, az1, r0, r1, lists)


def middle_kernel(par, q, m, own, lists, tables, ga0, ga1, gr0, gr1, s, matrix, own2, az0, az1, r0, r1, placed):
    matrix[...] = mortar_matrix(lists[...], ga_lists(par, ga0, ga1), tables[...])
    mortar = mortar_terms(par, matrix[...], own, ga0, ga1, placed)
    az, rad = outsides(par, ga0, ga1, gr0, gr1)

    def write(f, i, j, k, value):
        if value is not None:
            s[pl.ds(row(f, i, j, k), 8), :] = value

    apply_operator(q, m, s, az, rad, mortar, lambda x, *at: x, write)
    pack_faces(s, par, own2, az0, az1, r0, r1, None)


def ga_lists(par, ga0, ga1):
    return jnp.where(par[0] == 0, ga0[pl.ds(144, 8), :], ga1[pl.ds(144, 8), :])


def last_kernel(par, q, s, m, own, matrix, ga0, ga1, gr0, gr1, out, acc, placed):
    mortar = mortar_terms(par, matrix[...], own, ga0, ga1, placed)
    az, rad = outsides(par, ga0, ga1, gr0, gr1)

    def write(f, i, j, k, value):
        at = pl.ds(row(f, i, j, k), 8)
        acc[at, :] = 0.5 * ((acc[at, :] if value is None else value) + q[at, :])

    apply_operator(s, m, acc, az, rad, mortar, lambda x, *at: x, write)
    for a in range(8):
        for c in (0, 128, 256):
            width = min(128, 320 - c)
            out[a, :, c : c + width] = acc[pl.ds(c * 8 + a, width, stride=8), :].T


def call(kernel, outs, scratch=()):
    vmem = pl.BlockSpec(memory_space=pltpu.VMEM)
    smem = pl.BlockSpec(memory_space=pltpu.SMEM)

    def run(par, *args):
        return pl.pallas_call(
            kernel,
            out_shape=[jax.ShapeDtypeStruct(s, f32) for s in outs],
            in_specs=[smem] + [vmem] * len(args),
            out_specs=[vmem] * len(outs),
            scratch_shapes=[pltpu.VMEM(s, f32) for s in scratch],
            compiler_params=pltpu.CompilerParams(vmem_limit_bytes=32 * 2**20),
        )(par, *args)

    return run


def exchange(az0, az1, r0, r1, sectors, blocks):
    both = ("azim", "radax")
    at = lambda a, r: (a % sectors) * blocks + r
    on0 = [(a, a ^ 1) for a in range(sectors)]
    on1 = [(a, (a + 1 if a % 2 else a - 1) % sectors) for a in range(sectors)]
    rad0 = [(r, r ^ 1) for r in range(blocks)]
    rad1 = []
    for a in range(sectors):
        for r in range(blocks):
            if r in (0, blocks - 1):
                rad1.append((at(a, r), at(a ^ 1, r)))
            else:
                rad1.append((at(a, r), at(a, r + 1 if r % 2 else r - 1)))
    g1 = lax.ppermute(r1, both, rad1)
    ga1 = lax.ppermute(az1, "azim", on1)
    g0 = lax.ppermute(r0, "radax", rad0)
    ga0 = lax.ppermute(az0, "azim", on0)
    return ga0, ga1, g0, g1


def shards(solution, metric, intersections, counts, projections):
    sectors, blocks = lax.axis_size("azim"), lax.axis_size("radax")
    azim, radax = lax.axis_index("azim"), lax.axis_index("radax")
    par = jnp.stack([azim % 2, radax % 2, radax, azim]).astype(jnp.int32)
    in_use = lax.broadcasted_iota(jnp.int32, (2, 8), 1) < counts[0][:, None]
    lists = jnp.concatenate([intersections[0], in_use[:, None].astype(jnp.int32)], axis=1)
    lists = lists.transpose(0, 2, 1).reshape(16, 4).astype(f32)
    lists = jnp.pad(lists, ((0, 0), (0, 124)))
    turned = jnp.concatenate([projections[:2], projections[2:].transpose(0, 1, 3, 2)], axis=0)
    tables = jnp.repeat(turned.transpose(1, 0, 2, 3).reshape(16, 64), 8, axis=1)
    tables = jnp.pad(tables, ((0, 112), (0, 0)))
    nat = solution.reshape(8, 128, 320)
    state = (2560, 128)
    faces = [(152, 128), (152, 128), (80, 128), (80, 128)]
    small = [(144, 128), (144, 128), (80, 128), (80, 128)]
    q, m, own, *sent = call(enter_kernel, [state, (24, 128), (128, 128)] + faces)(
        par, nat, metric.reshape(8, 128, 3), lists
    )
    got = exchange(*sent, sectors, blocks)
    s, matrix, own2, *sent = call(
        middle_kernel, [state, (64, 128), (128, 128)] + small, [(64, 256)]
    )(par, q, m, own, lists, tables, *got)
    got = exchange(*sent, sectors, blocks)
    (out,) = call(last_kernel, [(8, 128, 320)], [state, (64, 256)])(par, q, s, m, own2, matrix, *got)
    return out.reshape(solution.shape)


def solution(mesh):
    in_specs = (
        P("azim", "radax", None, None),
        P("azim", "radax", None, None),
        P("azim", None, None, None),
        P("azim", None),
        P(),
    )
    out_specs = P("azim", "radax", None, None)
    return jax.shard_map(shards, mesh=mesh, in_specs=in_specs, out_specs=out_specs, check_vma=False)
```

profile of v0, /device:TPU:16, one launch (start us, length us, event | category | flops | bytes accessed | tf_op | source)
XLA Modules:
  0.0 46.1 jit_solution(5957393985449934776)
XLA Ops:
  0.0 0.0 copy-start.1
  0.0 0.7 %compare_convert_fusion = s32[2,1,8]{2,0,1:T(2,128)S(1)} fusion(s32[2]{0:T(128)} %bitcast.24), kind=kLoop, calls=%fused_computation.5 | loop fusion | flops 32 | bytes 72 | tf_op jit(solution)/shard_map/convert_element_type | solution.py:357
  0.7 0.7 %fusion = f32[2,8,4]{1,0,2:T(2,128)S(1)} fusion(s32[2,1,8]{2,0,1:T(2,128)S(1)} %compare_convert_fusion, s32[2,3,8]{2,0,1:T(2,128)} %bitcast.23), kind=kLoop, calls=%fused_computation.4 | loop fusion | flops 128 | bytes 512 | tf_op jit(solution)/shard_map/convert_element_type | solution.py:358
  1.4 0.1 copy.14
  1.5 1.3 %copy.9 = f32[8,8,16,3]{3,2,1,0:T(8,128)S(1)} copy(f32[8,8,16,3]{2,1,3,0:T(8,128)} %param.6) | data formatting | bytes 24576 | tf_op args[1]
  2.9 0.1 pad_add_fusion.par
  2.9 0.0 copy-start
  2.9 1.4 %copy-done = f32[8,8,16,320]{3,2,1,0:T(8,128)S(1)} copy-done((f32[8,8,16,320]{3,2,1,0:T(8,128)S(1)}, f32[8,8,16,320]{3,2,1,0:T(8,128)}, u32[]{:S(2)}) %copy-start) | copy-done | bytes 1310744
  4.4 1.5 %shard_map.55 = (f32[2560,128]{1,0:T(8,128)S(1)}, f32[24,128]{1,0:T(8,128)S(1)}, f32[128,128]{1,0:T(8,128)S(1)}, f32[152,128]{1,0:T(8,128)S(1)}, f32[152,128]{1,...) custom-call(s32[4]{0:T(128)S(1)} %pad_add_fusion.par, f32[8,128,320]{2,1,0:T(8,128)S(1)} %bitcast.20, ...), custom_call_target="tpu_custom_call" | custom-call | tf_op jit(solution)/shard_map/pallas_call | solution.py:320
  5.9 1.6 %collective-permute-start.2 = (f32[80,128]{1,0:T(8,128)S(1)}, f32[80,128]{1,0:T(8,128)S(1)}, u32[]{:S(2)}, u32[]{:S(2)}) collective-permute-start(f32[80,128]{1,0:T(8,128)S(1)} %get-tuple-element.24), channel_id=1, source_target_pairs={{0,1},{1,0},{2,3},{3,2},{4,5},{5,4},{6,7},{7,6},{8,9},{9,8},{10,11... | collective-permute-start | bytes 122888 | tf_op jit(solution)/shard_map/ppermute | solution.py:347
  7.5 1.9 %collective-permute-start.3 = (f32[80,128]{1,0:T(8,128)S(1)}, f32[80,128]{1,0:T(8,128)S(1)}, u32[]{:S(2)}, u32[]{:S(2)}) collective-permute-start(f32[80,128]{1,0:T(8,128)S(1)} %get-tuple-element.25), channel_id=1, source_target_pairs={{0,8},{1,2},{2,1},{3,4},{4,3},{5,6},{6,5},{7,15},{8,0},{9,10},{10,... | collective-permute-start | bytes 122888 | tf_op jit(solution)/shard_map/ppermute | solution.py:345
  9.3 0.0 collective-permute-start
  9.3 7.6 %collective-permute-start.1 = (f32[152,128]{1,0:T(8,128)S(1)}, f32[152,128]{1,0:T(8,128)S(1)}, u32[]{:S(2)}, u32[]{:S(2)}) collective-permute-start(f32[152,128]{1,0:T(8,128)S(1)} %get-tuple-element.23), channel_id=1, source_target_pairs={{0,248},{8,16},{16,8},{24,32},{32,24},{40,48},{48,40},{56,64},{64,... | collective-permute-start | bytes 233480 | tf_op jit(solution)/shard_map/ppermute | solution.py:346
  16.9 0.0 copy-done.1
  17.0 0.1 copy.13
  17.1 0.0 collective-permute-done.2.gr0
  17.2 0.0 collective-permute-done.3.gr1
  17.2 0.0 collective-permute-done.ga0
  17.2 1.8 %collective-permute-done.1.ga1 = f32[152,128]{1,0:T(8,128)S(1)} collective-permute-done((f32[152,128]{1,0:T(8,128)S(1)}, f32[152,128]{1,0:T(8,128)S(1)}, u32[]{:S(2)}, u32[]{:S(2)}) %collective-permute-start.1) | collective-permute-done | bytes 77856 | tf_op jit(solution)/shard_map/ppermute | solution.py:346
  19.0 7.0 %shard_map.56 = (f32[2560,128]{1,0:T(8,128)S(1)}, f32[64,128]{1,0:T(8,128)S(1)}, f32[128,128]{1,0:T(8,128)S(1)}, f32[144,128]{1,0:T(8,128)S(1)}, f32[144,128]{1,...) custom-call(s32[4]{0:T(128)S(1)} %pad_add_fusion.par, f32[2560,128]{1,0:T(8,128)S(1)} %get-tuple-element.19.q, ...), custom_call_target="tpu_custom_call" | custom-call | tf_op jit(solution)/shard_map/pallas_call | solution.py:320
  26.1 0.1 collective-permute-start.4
  26.2 3.9 %collective-permute-start.5 = (f32[144,128]{1,0:T(8,128)S(1)}, f32[144,128]{1,0:T(8,128)S(1)}, u32[]{:S(2)}, u32[]{:S(2)}) collective-permute-start(f32[144,128]{1,0:T(8,128)S(1)} %get-tuple-element.30), channel_id=1, source_target_pairs={{0,248},{8,16},{16,8},{24,32},{32,24},{40,48},{48,40},{56,64},{64,... | collective-permute-start | bytes 221192 | tf_op jit(solution)/shard_map/ppermute | solution.py:346
  30.1 0.0 collective-permute-start.6
  30.1 2.3 %collective-permute-start.7 = (f32[80,128]{1,0:T(8,128)S(1)}, f32[80,128]{1,0:T(8,128)S(1)}, u32[]{:S(2)}, u32[]{:S(2)}) collective-permute-start(f32[80,128]{1,0:T(8,128)S(1)} %get-tuple-element.32), channel_id=1, source_target_pairs={{0,8},{1,2},{2,1},{3,4},{4,3},{5,6},{6,5},{7,15},{8,0},{9,10},{10,... | collective-permute-start | bytes 122888 | tf_op jit(solution)/shard_map/ppermute | solution.py:345
  32.4 1.7 %collective-permute-done.6.gr0 = f32[80,128]{1,0:T(8,128)S(1)} collective-permute-done((f32[80,128]{1,0:T(8,128)S(1)}, f32[80,128]{1,0:T(8,128)S(1)}, u32[]{:S(2)}, u32[]{:S(2)}) %collective-permute-start.6) | collective-permute-done | bytes 40992 | tf_op jit(solution)/shard_map/ppermute | solution.py:347
  34.1 3.6 %collective-permute-done.7.gr1 = f32[80,128]{1,0:T(8,128)S(1)} collective-permute-done((f32[80,128]{1,0:T(8,128)S(1)}, f32[80,128]{1,0:T(8,128)S(1)}, u32[]{:S(2)}, u32[]{:S(2)}) %collective-permute-start.7) | collective-permute-done | bytes 40992 | tf_op jit(solution)/shard_map/ppermute | solution.py:345
  37.7 0.0 collective-permute-done.4.ga0
  37.7 0.0 collective-permute-done.5.ga1
  37.7 8.4 %shard_map.57 = f32[8,128,320]{2,1,0:T(8,128)} custom-call(s32[4]{0:T(128)S(1)} %pad_add_fusion.par, f32[2560,128]{1,0:T(8,128)S(1)} %get-tuple-element.19.q, f32[2560,128]{1,0:T(8,128)S(1)} %get-tuple-element.26.s, f32[24,128]{1,0:T(8,128)S(1)} %get-tuple-element.20.m, f32[128,128]{1,0:T(8,128)S(1)} %get-tuple-element.27.own, ...), custom_call_target="tpu_custom_call" | custom-call | tf_op jit(solution)/shard_map/pallas_call | solution.py:320
  (7 shorter events, 0.1 us)
Async XLA Ops:
  0.0 16.9 %copy-start.1 = (f32[4,16,4,4]{1,3,2,0:T(4,128)S(1)}, f32[4,16,4,4]{1,3,2,0:T(4,128)}, u32[]{:S(2)}) copy-start(f32[4,16,4,4]{1,3,2,0:T(4,128)} %param.9) | copy-start | bytes 12292
  2.9 1.4 %copy-start = (f32[8,8,16,320]{3,2,1,0:T(8,128)S(1)}, f32[8,8,16,320]{3,2,1,0:T(8,128)}, u32[]{:S(2)}) copy-start(f32[8,8,16,320]{3,2,1,0:T(8,128)} %param.5) | copy-start | bytes 3932164
  5.9 11.3 %collective-permute-start.2 = (f32[80,128]{1,0:T(8,128)S(1)}, f32[80,128]{1,0:T(8,128)S(1)}, u32[]{:S(2)}, u32[]{:S(2)}) collective-permute-start(f32[80,128]{1,0:T(8,128)S(1)} %get-tuple-element.24), channel_id=1, source_target_pairs={{0,1},{1,0},{2,3},{3,2},{4,5},{5,4},{6,7},{7,6},{8,9},{9,8},{10,11... | collective-permute-start | bytes 122888 | tf_op jit(solution)/shard_map/ppermute | solution.py:347
  7.5 9.7 %collective-permute-start.3 = (f32[80,128]{1,0:T(8,128)S(1)}, f32[80,128]{1,0:T(8,128)S(1)}, u32[]{:S(2)}, u32[]{:S(2)}) collective-permute-start(f32[80,128]{1,0:T(8,128)S(1)} %get-tuple-element.25), channel_id=1, source_target_pairs={{0,8},{1,2},{2,1},{3,4},{4,3},{5,6},{6,5},{7,15},{8,0},{9,10},{10,... | collective-permute-start | bytes 122888 | tf_op jit(solution)/shard_map/ppermute | solution.py:345
  9.3 7.8 %collective-permute-start = (f32[152,128]{1,0:T(8,128)S(1)}, f32[152,128]{1,0:T(8,128)S(1)}, u32[]{:S(2)}, u32[]{:S(2)}) collective-permute-start(f32[152,128]{1,0:T(8,128)S(1)} %get-tuple-element.22), channel_id=1, source_target_pairs={{0,8},{8,0},{16,24},{24,16},{32,40},{40,32},{48,56},{56,48},{64,72... | collective-permute-start | bytes 233480 | tf_op jit(solution)/shard_map/ppermute | solution.py:348
  9.3 9.7 %collective-permute-start.1 = (f32[152,128]{1,0:T(8,128)S(1)}, f32[152,128]{1,0:T(8,128)S(1)}, u32[]{:S(2)}, u32[]{:S(2)}) collective-permute-start(f32[152,128]{1,0:T(8,128)S(1)} %get-tuple-element.23), channel_id=1, source_target_pairs={{0,248},{8,16},{16,8},{24,32},{32,24},{40,48},{48,40},{56,64},{64,... | collective-permute-start | bytes 233480 | tf_op jit(solution)/shard_map/ppermute | solution.py:346
  26.1 11.7 %collective-permute-start.4 = (f32[144,128]{1,0:T(8,128)S(1)}, f32[144,128]{1,0:T(8,128)S(1)}, u32[]{:S(2)}, u32[]{:S(2)}) collective-permute-start(f32[144,128]{1,0:T(8,128)S(1)} %get-tuple-element.29), channel_id=1, source_target_pairs={{0,8},{8,0},{16,24},{24,16},{32,40},{40,32},{48,56},{56,48},{64,72... | collective-permute-start | bytes 221192 | tf_op jit(solution)/shard_map/ppermute | solution.py:348
  26.2 11.6 %collective-permute-start.5 = (f32[144,128]{1,0:T(8,128)S(1)}, f32[144,128]{1,0:T(8,128)S(1)}, u32[]{:S(2)}, u32[]{:S(2)}) collective-permute-start(f32[144,128]{1,0:T(8,128)S(1)} %get-tuple-element.30), channel_id=1, source_target_pairs={{0,248},{8,16},{16,8},{24,32},{32,24},{40,48},{48,40},{56,64},{64,... | collective-permute-start | bytes 221192 | tf_op jit(solution)/shard_map/ppermute | solution.py:346
  30.1 4.0 %collective-permute-start.6 = (f32[80,128]{1,0:T(8,128)S(1)}, f32[80,128]{1,0:T(8,128)S(1)}, u32[]{:S(2)}, u32[]{:S(2)}) collective-permute-start(f32[80,128]{1,0:T(8,128)S(1)} %get-tuple-element.31), channel_id=1, source_target_pairs={{0,1},{1,0},{2,3},{3,2},{4,5},{5,4},{6,7},{7,6},{8,9},{9,8},{10,11... | collective-permute-start | bytes 122888 | tf_op jit(solution)/shard_map/ppermute | solution.py:347
  30.1 7.6 %collective-permute-start.7 = (f32[80,128]{1,0:T(8,128)S(1)}, f32[80,128]{1,0:T(8,128)S(1)}, u32[]{:S(2)}, u32[]{:S(2)}) collective-permute-start(f32[80,128]{1,0:T(8,128)S(1)} %get-tuple-element.32), channel_id=1, source_target_pairs={{0,8},{1,2},{2,1},{3,4},{4,3},{5,6},{6,5},{7,15},{8,0},{9,10},{10,... | collective-permute-start | bytes 122888 | tf_op jit(solution)/shard_map/ppermute | solution.py:345
where the time goes:
time: 46.3 us; the launch traced here: 46.1 us
  starting transfers between devices  17.3 us (37%)
  Pallas kernels  16.9 us (37%)
  waiting for transfers between devices  7.19 us (16%)
  local copies, waits for them, and re-layouts  3.01 us (7%)
  other arithmetic  1.51 us (3%)
    pallas_call x3, Pallas kernels, run(): pl.pallas_call(kernel, out_shape=[jax.ShapeDtypeStruct(s, f32) for s in o...  16.9 us
    ppermute x2, starting transfers between devices, exchange(): ga1 = lax.ppermute(az1, 'azim', on1)  11.5 us
    ppermute x2, starting transfers between devices, exchange(): g1 = lax.ppermute(r1, both, rad1)  4.14 us
    ppermute x2, waiting for transfers between devices, exchange(): g1 = lax.ppermute(r1, both, rad1)  3.62 us
    unnamed x6, local copies, waits for them, and re-layouts  2.75 us
    ppermute x2, waiting for transfers between devices, exchange(): ga1 = lax.ppermute(az1, 'azim', on1)  1.84 us
    ppermute x2, waiting for transfers between devices, exchange(): g0 = lax.ppermute(r0, 'radax', rad0)  1.73 us
    ppermute x2, starting transfers between devices, exchange(): g0 = lax.ppermute(r0, 'radax', rad0)  1.58 us
  transfers between devices with their start and end apart: 8, of which 3 were waited for; matrix products, arithmetic and copies ran while one was open for 0% of the time, Pallas kernels for 0%

commit v1 on v0

v1 whole, which is shorter than its diff:
```python
import functools
import jax
import jax.numpy as jnp
import numpy as np
from jax import lax
from jax.experimental import pallas as pl
from jax.experimental.pallas import tpu as pltpu
from jax.sharding import PartitionSpec as P

time_step = 0.02
mean_flow = (0.5, 0.0, 0.4)
speeds = tuple(abs(u) + 1.0 for u in mean_flow)
highest = lax.Precision.HIGHEST
f32 = jnp.float32


def line_numbers():
    points = np.array([-1.0, -1.0 / np.sqrt(5.0), 1.0 / np.sqrt(5.0), 1.0])
    barycentric = np.array(
        [1.0 / np.prod([points[j] - points[k] for k in range(4) if k != j]) for j in range(4)]
    )
    single = np.zeros((4, 4))
    for i in range(4):
        for j in range(4):
            if i != j:
                single[i, j] = barycentric[j] / barycentric[i] / (points[i] - points[j])
        single[i, i] = -np.sum(single[i])
    return single


D = line_numbers()


def row(f, i, j, k):
    return (f * 64 + 16 * i + 4 * j + k) * 8


def tile(ref, f, i, j, k):
    return ref[pl.ds(row(f, i, j, k), 8), :]


def lane_ids():
    return lax.broadcasted_iota(jnp.int32, (8, 128), 1)


def minus_slope(x, scale):
    e0, e1 = x[0] - x[3], x[1] - x[2]
    t = (x[0] + x[3]) - (x[1] + x[2])
    c = -scale * 0.5
    outer = (c * (D[0, 0] - D[0, 3])) * e0 + (c * (D[0, 1] - D[0, 2])) * e1
    inner = (c * (D[1, 0] - D[1, 3])) * e0 + (c * (D[1, 1] - D[1, 2])) * e1
    outer_t = (c * (D[0, 0] + D[0, 3])) * t
    inner_t = (c * (D[1, 0] + D[1, 3])) * t
    return [outer + outer_t, inner + inner_t, inner - inner_t, outer - outer_t]


def line_terms(d, x, low, high):
    flow, speed = mean_flow[d], speeds[d]
    w0 = [3.0 * v for v in low]
    w3 = [3.0 * v for v in high]
    mine = 1 + d
    slopes = {}
    for f in (mine, 4):
        h = minus_slope(x[f], 1.0)
        h[0] = h[0] + w0[f]
        h[3] = h[3] - w3[f]
        slopes[f] = h
    result = []
    for f in range(5):
        if f == mine:
            r = [slopes[4][i] + flow * slopes[mine][i] if flow else slopes[4][i] for i in range(4)]
            r[0] = r[0] + speed * w0[f]
            r[3] = r[3] + speed * w3[f]
        elif f == 4:
            r = [slopes[mine][i] + flow * slopes[4][i] if flow else slopes[mine][i] for i in range(4)]
            r[0] = r[0] + speed * w0[f]
            r[3] = r[3] + speed * w3[f]
        else:
            r = minus_slope(x[f], flow) if flow else [None] * 4
            if f == 0:
                r = [slopes[mine][i] if r[i] is None else r[i] + slopes[mine][i] for i in range(4)]
            lows, highs = (speed + flow) * w0[f], (speed - flow) * w3[f]
            r[0] = lows if r[0] is None else r[0] + lows
            r[3] = highs if r[3] is None else r[3] + highs
        result.append(r)
    return result


def position():
    azim, radax = lax.axis_index("azim"), lax.axis_index("radax")
    return azim & 1, radax & 1, radax


def staged(lines, fetch, finish):
    ready = fetch(*lines[0])
    for at, line in enumerate(lines):
        later = fetch(*lines[at + 1]) if at + 1 < len(lines) else None
        finish(*line, *ready)
        ready = later


def pairs():
    return [(p, r) for p in range(4) for r in range(4)]


def inner_operator(q, m, acc, first):
    lanes = lane_ids()
    sub = lax.broadcasted_iota(jnp.int32, (8, 128), 0)
    axial = lanes & 15

    def passes(d, nodes, low_of, high_of, put):
        scale = m[pl.ds(8 * d, 8), :]

        def fetch(p, r):
            low, high = [], []
            for f in range(5):
                x0, x3 = tile(q, f, *nodes(p, r, 0)), tile(q, f, *nodes(p, r, 3))
                low.append(low_of(x0, x3))
                high.append(high_of(x0, x3))
            return low, high

        def finish(p, r, low, high):
            x = [[tile(q, f, *nodes(p, r, e)) for e in range(4)] for f in range(5)]
            terms = line_terms(d, x, low, high)
            for f in range(5):
                for e in range(4):
                    if terms[f][e] is not None:
                        put(f, *nodes(p, r, e), x[f][e], scale * terms[f][e])

        staged(pairs(), fetch, finish)

    def begin(f, i, j, k, x, term):
        acc[pl.ds(row(f, i, j, k), 8), :] = first(x, f, i, j, k) + term

    def add(f, i, j, k, x, term):
        at = pl.ds(row(f, i, j, k), 8)
        acc[at, :] = acc[at, :] + term

    def axial_low(x0, x3):
        outside = jnp.where(axial == 0, 0.0, pltpu.roll(x3, 1, 1))
        return jnp.where(axial == 8, 0.0, outside - x0)

    def axial_high(x0, x3):
        outside = jnp.where(axial == 15, 0.0, pltpu.roll(x0, 127, 1))
        return jnp.where(axial == 7, 0.0, outside - x3)

    passes(2, lambda i, j, k: (i, j, k), axial_low, axial_high, begin)
    passes(
        0,
        lambda j, k, i: (i, j, k),
        lambda x0, x3: jnp.where(sub == 0, 0.0, pltpu.roll(x3, 1, 0) - x0),
        lambda x0, x3: jnp.where(sub == 7, 0.0, pltpu.roll(x0, 7, 0) - x3),
        add,
    )
    passes(
        1,
        lambda i, k, j: (i, j, k),
        lambda x0, x3: jnp.where(lanes < 16, 0.0, pltpu.roll(x3, 16, 1) - x0),
        lambda x0, x3: jnp.where(lanes >= 112, 0.0, pltpu.roll(x0, 112, 1) - x3),
        add,
    )


def coupled(f, d):
    return 4 if f == 1 + d else 1 + d if f in (0, 4) else None


def end_terms(q, m, base, acc, factor, fields, sides):
    for f in fields:
        for i, j in pairs():
            at = pl.ds(row(f, i, j, 1), 16)
            acc[at, :] = base[at, :]
    for d, nodes in (
        (2, lambda i, j, k: (i, j, k)),
        (0, lambda j, k, i: (i, j, k)),
        (1, lambda i, k, j: (i, j, k)),
    ):
        scale = (3.0 * factor) * m[pl.ds(8 * d, 8), :]
        flow, speed = mean_flow[d], speeds[d]
        old = base if d == 2 else acc
        needed = sorted(set(fields) | {coupled(f, d) for f in fields} - {None})

        def fetch(p, r):
            return ({f: sides[d](f, p, r, tile(q, f, *nodes(p, r, 0)), tile(q, f, *nodes(p, r, 3))) for f in needed},)

        def finish(p, r, jumps):
            for f in fields:
                other = coupled(f, d)
                for end, sign in ((0, 1.0), (1, -1.0)):
                    term = (speed + sign * flow) * jumps[f][end]
                    if other is not None:
                        term = term + jumps[other][end] if end == 0 else term - jumps[other][end]
                    at = pl.ds(row(f, *nodes(p, r, 3 * end)), 8)
                    acc[at, :] = old[at, :] + scale * term

        staged(pairs(), fetch, finish)


def pack_sector(q, side, message):
    spot = (lane_ids() + side) & 15
    for f in range(5):
        low = q[pl.ds(f * 64 * 8, 16, stride=8), :]
        high = q[pl.ds((f * 64 + 48) * 8 + 7, 16, stride=8), :]
        message[pl.ds(f * 16, 16), :] = jnp.where(side == 0, low, high)
    for i in range(4):
        for block, fields in ((0, range(4)), (1, (4,))):
            packed = jnp.zeros((8, 128), f32)
            for f in fields:
                for j in range(4):
                    p = 4 * (f % 4) + j
                    at = pl.multiple_of(row(f, i, j, 0) + 24 * side, 8)
                    packed = jnp.where(spot == p, pltpu.roll(q[pl.ds(at, 8), :], (120 + p) % 128, 1), packed)
            message[pl.ds(80 + block * 32 + i * 8, 8), :] = pltpu.roll(packed, side, 1)


def pack_blocks(q, side, message):
    place = ((lane_ids() >> 4) + side) & 7
    for g in range(10):
        packed = jnp.zeros((8, 128), f32)
        for p in range(8):
            f, n = divmod(g * 8 + p, 16)
            i, k = divmod(n, 4)
            at = pl.multiple_of(row(f, i, 0, k) + 96 * side, 8)
            packed = jnp.where(place == p, pltpu.roll(q[pl.ds(at, 8), :], 16 * p, 1), packed)
        message[pl.ds(g * 8, 8), :] = pltpu.roll(packed, 16 * side, 1)


def choose(par, ga0, ga1, gr0, gr1, back, ahead, below, above):
    even = par[0] == 0
    outward = par[1] == 0
    rows = back.shape[0]
    one, two = ga0[pl.ds(0, rows), :], ga1[pl.ds(0, rows), :]
    back[...] = jnp.where(even, two, one)
    ahead[...] = jnp.where(even, one, two)
    one, two = gr0[pl.ds(0, 80), :], gr1[pl.ds(0, 80), :]
    below[...] = jnp.where(par[2] == 0, 0.0, jnp.where(outward, two, one))
    above[...] = jnp.where(par[2] == 7, 0.0, jnp.where(outward, one, two))


def outside_jumps(back, ahead, below, above, by_rows, mortar):
    sub = lax.broadcasted_iota(jnp.int32, (8, 128), 0)
    lanes = lane_ids()
    axial = lanes & 15

    def az(f, j, k, x0, x3):
        at = pl.ds(f * 16 + 4 * j + k, 1)
        return jnp.where(sub == 0, back[at, :] - x0, 0.0), jnp.where(sub == 7, ahead[at, :] - x3, 0.0)

    def rad(f, i, k, x0, x3):
        n = f * 16 + 4 * i + k
        if by_rows:
            at = pl.ds(n, 1)
            before = pltpu.roll(jnp.broadcast_to(below[at, :], (8, 128)), 16, 1, stride=16, stride_axis=0)
            after = pltpu.roll(jnp.broadcast_to(above[at, :], (8, 128)), 0, 1, stride=16, stride_axis=0)
        else:
            g, p = divmod(n, 8)
            at = pl.ds(g * 8, 8)
            before = pltpu.roll(below[at, :], (128 - 16 * p) % 128, 1)
            after = pltpu.roll(above[at, :], (112 - 16 * p) % 128, 1)
        return jnp.where(lanes < 16, before - x0, 0.0), jnp.where(lanes >= 112, after - x3, 0.0)

    def ax(f, i, j, x0, x3):
        to_stator, to_rotor = mortar(f, i, j)
        return jnp.where(axial == 8, to_stator, 0.0), jnp.where(axial == 7, to_rotor, 0.0)

    return {0: az, 1: rad, 2: ax}


def mortar_matrix(lists, following, tables):
    own, later = lists.T, following.T

    def column(t):
        return jnp.concatenate([own[0:8, t : t + 1], own[0:8, t + 3 : t + 4], later[0:8, t : t + 1]], axis=0)

    rotor, stator, kind = (column(t) for t in range(3))
    slot = lax.broadcasted_iota(jnp.int32, (24, 1), 0)
    filled = jnp.concatenate(
        [
            jnp.broadcast_to(lists[6:7, 0:1], (8, 1)),
            jnp.broadcast_to(lists[7:8, 0:1], (8, 1)),
            jnp.broadcast_to(following[6:7, 0:1], (8, 1)),
        ],
        axis=0,
    )
    used = ((slot & 7).astype(f32) < filled).astype(f32)
    lanes = lax.broadcasted_iota(jnp.int32, (24, 128), 1)
    pick = (lanes.astype(f32) == kind).astype(f32)
    face = (lanes & 7).astype(f32)
    on_rotor = (face == rotor).astype(f32)
    on_stator = (face == stator).astype(f32) * 1.0
    entries = jnp.dot(pick, tables, precision=highest, preferred_element_type=f32)
    order = lax.broadcasted_iota(jnp.int32, (24, 128), 0)
    p_rot = entries[:, 0:128] * on_rotor
    p_sta = -entries[:, 128:256] * on_stator
    q_rot = -entries[:, 256:384] * on_rotor * used
    q_sta = entries[:, 384:512] * on_stator * used
    first = (order < 8).astype(f32)
    third = (order >= 16).astype(f32)
    b_parts = [p_rot * first, p_rot * (1.0 - first), p_sta * (1.0 - third), p_sta * third]
    c_parts = [q_sta * (1.0 - third), q_rot * (1.0 - first)]
    b_all = jnp.concatenate(
        [jnp.concatenate([b[:, 32 * m : 32 * m + 32] for b in b_parts], axis=1) for m in range(4)], axis=0
    )
    c_all = jnp.concatenate(
        [jnp.concatenate([c[:, 32 * m : 32 * m + 32] for c in c_parts], axis=1) for m in range(4)], axis=0
    )
    return lax.dot_general(
        c_all, b_all, (((0,), (0,)), ((), ())), precision=highest, preferred_element_type=f32
    )


def mortar_terms(par, matrix, s0, s1, back, ahead, placed):
    even = par[0] == 0
    blocks = []
    for block in range(2):
        at = pl.ds(80 + block * 32, 32)
        one, two = s0[at, :], s1[at, :]
        mine, yours = jnp.where(even, one, two), jnp.where(even, two, one)
        blocks.append(jnp.concatenate([back[at, :], mine, yours, ahead[at, :]], axis=0))
    traces = jnp.concatenate(blocks, axis=1)
    placed[...] = jnp.dot(matrix, traces, precision=highest, preferred_element_type=f32)

    def mortar(f, i, j):
        block, p = divmod(4 * f + j, 16)
        at = pl.ds(128 * block, 128)
        to_stator = pltpu.roll(placed[pl.ds(8 * i, 8), at], (8 - p) % 128, 1)
        to_rotor = pltpu.roll(placed[pl.ds(32 + 8 * i, 8), at], (7 - p) % 128, 1)
        return to_stator, to_rotor

    return mortar


def rim_kernel(state, r0, r1, rims, sems):
    par = position()
    copies = [pltpu.make_async_copy(state.at[:, 7 * e], rims.at[e], sems.at[e]) for e in range(2)]
    for copy in copies:
        copy.start()
    for e in range(2):
        copies[e].wait()
    even = par[1] == 0
    for c in (0, 128, 256):
        width = min(128, 320 - c)
        low, high = (
            jnp.concatenate([rims[e, 7 - a, :, c : c + width] for a in range(8)], axis=0).T for e in range(2)
        )
        for g in range(width // 16):
            at = 16 * g
            down, up = low[at : at + 4], high[at + 12 : at + 16]
            r1[pl.ds(c // 4 + 4 * g, 4), :] = jnp.where(even, down, up)
            r0[pl.ds(c // 4 + 4 * g, 4), :] = jnp.where(even, up, down)


def enter_kernel(counts, nat, slots, q, s1):
    par = position()
    for a in range(8):
        for c in (0, 128, 256):
            width = min(128, 320 - c)
            q[pl.ds(c * 8 + a, width, stride=8), :] = nat[a, :, c : c + width].T
    pack_sector(q, par[0], s1)
    lists = jnp.concatenate(
        [
            jnp.concatenate([slots[b].astype(f32) for b in range(2)], axis=0),
            jnp.concatenate(
                [jnp.broadcast_to(counts[:, b : b + 1].astype(f32), (1, 8)) for b in range(2)], axis=0
            ),
        ],
        axis=0,
    )
    s1[pl.ds(144, 8), :] = jnp.concatenate([lists, jnp.zeros((8, 120), f32)], axis=1)


def others_kernel(q, s1, s0):
    par = position()
    pack_sector(q, 1 - par[0], s0)
    s0[pl.ds(144, 8), :] = s1[pl.ds(144, 8), :]


def inner_kernel(q, m, acc):
    inner_operator(q, m, acc, lambda x, *at: x)


def middle_kernel(
    inner, q, m, s0, s1, tables, ga0, ga1, gr0, gr1, s, matrix, r1, placed, back, ahead, below, above
):
    par = position()
    choose(par, ga0, ga1, gr0, gr1, back, ahead, below, above)
    matrix[...] = mortar_matrix(s1[pl.ds(144, 8), :], ahead[pl.ds(144, 8), :], tables[...])
    mortar = mortar_terms(par, matrix[...], s0, s1, back, ahead, placed)
    end_terms(q, m, inner, s, 1.0, range(5), outside_jumps(back, ahead, below, above, True, mortar))
    pack_blocks(s, par[1], r1)
    r1[pl.ds(80, 72), :] = jnp.zeros((72, 128), f32)


def sector_kernel(s, s1):
    par = position()
    pack_sector(s, par[0], s1)


def later_kernel(s, s0, r0):
    par = position()
    pack_blocks(s, 1 - par[1], r0)
    pack_sector(s, 1 - par[0], s0)


def inner_last_kernel(s, m, q, acc):
    half = {8 * d: 0.5 * m[pl.ds(8 * d, 8), :] for d in range(3)}

    class Halved:
        def __getitem__(self, at):
            return half[at[0].start]

    inner_operator(s, Halved(), acc, lambda x, *at: 0.5 * (x + tile(q, *at)))


def last_kernel(
    inner, s, m, s0, s1, matrix, ga0, ga1, gr0, gr1, out, acc, placed, back, ahead, below, above, turned, sems
):
    par = position()
    choose(par, ga0, ga1, gr0, gr1, back, ahead, below, above)
    mortar = mortar_terms(par, matrix[...], s0, s1, back, ahead, placed)
    jumps = outside_jumps(back, ahead, below, above, False, mortar)
    copies = []
    for c, fields in ((128, (2, 3)), (0, (0, 1)), (256, (4,))):
        width = min(128, 320 - c)
        end_terms(s, m, inner, acc, 0.5, fields, jumps)
        for a in range(8):
            turned[a, :, c : c + width] = acc[pl.ds(c * 8 + a, width, stride=8), :].T
            copies.append(
                pltpu.make_async_copy(
                    turned.at[a, :, pl.ds(c, width)], out.at[a, :, pl.ds(c, width)], sems.at[len(copies)]
                )
            )
            copies[-1].start()
    for copy in copies:
        copy.wait()


def call(kernel, outs, scratch=(), where={}, out_where=pltpu.VMEM, limit=32, cost=1):
    def run(*args):
        return pl.pallas_call(
            kernel,
            out_shape=[jax.ShapeDtypeStruct(s, f32) for s in outs],
            in_specs=[pl.BlockSpec(memory_space=where.get(n, pltpu.VMEM)) for n in range(len(args))],
            out_specs=[pl.BlockSpec(memory_space=out_where)] * len(outs),
            scratch_shapes=[s if not isinstance(s, tuple) else pltpu.VMEM(s, f32) for s in scratch],
            compiler_params=pltpu.CompilerParams(vmem_limit_bytes=limit * 2**20),
            cost_estimate=pl.CostEstimate(flops=0, transcendentals=0, bytes_accessed=cost * 3_000_000),
        )(*args)

    return run


def pairings(sectors, blocks):
    at = lambda a, r: (a % sectors) * blocks + r
    az0 = [(a, a ^ 1) for a in range(sectors)]
    az1 = [(a, (a + 1 if a % 2 else a - 1) % sectors) for a in range(sectors)]
    rad0 = [(r, r ^ 1) for r in range(blocks)]
    rad1 = []
    for a in range(sectors):
        for r in range(blocks):
            if r in (0, blocks - 1):
                rad1.append((at(a, r), at(a ^ 1, r)))
            else:
                rad1.append((at(a, r), at(a, r + 1 if r % 2 else r - 1)))
    return az0, az1, rad0, rad1


def shards(solution, metric, intersections, counts, projections):
    sectors, blocks = lax.axis_size("azim"), lax.axis_size("radax")
    az0, az1, rad0, rad1 = pairings(sectors, blocks)

    def across(r0, r1, s0, s1):
        gr1 = lax.ppermute(r1, ("azim", "radax"), rad1)
        gs1 = lax.ppermute(s1, "azim", az1)
        gr0 = lax.ppermute(r0, "radax", rad0)
        gs0 = lax.ppermute(s0, "azim", az0)
        return gs0, gs1, gr0, gr1

    state, rim, trace, first_trace = (2560, 128), (80, 128), (144, 128), (152, 128)
    dma = pltpu.SemaphoreType.DMA
    r0, r1 = call(rim_kernel, [rim, rim], [(2, 8, 16, 320), dma((2,))], {0: pltpu.HBM}, limit=53)(solution)
    turned = jnp.concatenate([projections[:2], projections[2:].transpose(0, 1, 3, 2)], axis=0)
    tables = jnp.repeat(turned.transpose(1, 0, 2, 3).reshape(16, 64), 8, axis=1)
    tables = jnp.pad(tables, ((0, 112), (0, 0)))
    m = time_step * metric.transpose(3, 0, 1, 2).reshape(24, 128)
    nat = solution.reshape(8, 128, 320)
    q, s1 = call(enter_kernel, [state, first_trace])(counts, nat, intersections[0])
    (s0,) = call(others_kernel, [first_trace])(q, s1)
    got = across(r0, r1, s0, s1)
    (inner,) = call(inner_kernel, [state])(q, m)
    sides = [(64, 256), first_trace, first_trace, rim, rim]
    s, matrix, r1 = call(middle_kernel, [state, (64, 128), first_trace], sides)(
        inner, q, m, s0, s1, tables, *got
    )
    (s1,) = call(sector_kernel, [trace])(s)
    s0, r0 = call(later_kernel, [trace, rim])(s)
    got = across(r0, r1, s0, s1)
    (inner,) = call(inner_last_kernel, [state])(s, m, q)
    sides = [state, (64, 256), trace, trace, rim, rim]
    (out,) = call(last_kernel, [(8, 128, 320)], sides + [(8, 128, 320), dma((24,))], {}, pltpu.HBM)(
        inner, s, m, s0, s1, matrix, *got
    )
    return out.reshape(solution.shape)


def solution(mesh):
    in_specs = (
        P("azim", "radax", None, None),
        P("azim", "radax", None, None),
        P("azim", None, None, None),
        P("azim", None),
        P(),
    )
    out_specs = P("azim", "radax", None, None)
    return jax.shard_map(shards, mesh=mesh, in_specs=in_specs, out_specs=out_specs, check_vma=False)
```

time: 46.3 us -> 28.9 us (0.62)
  Pallas kernels: 16.9 us -> 9 us
  waiting for transfers between devices: 7.19 us -> 2.86 us
  local copies, waits for them, and re-layouts: 3.01 us -> 0.27 us
  other arithmetic: 1.51 us -> 0.02 us
  starting transfers between devices: 17.3 us -> 16.4 us
    pallas_call x3 -> x9, Pallas kernels: 16.9 us -> 9 us  [run(): pl.pallas_call(kernel, out_shape=[jax.ShapeDtypeStruct(s, f32) for s in o...]
    ppermute x8, waiting for transfers between devices: 7.19 us -> 2.86 us  [the longest x2 2.59 us: across(): gr0 = lax.ppermute(r0, 'radax', rad0)]
    unnamed x6 -> x11, local copies, waits for them, and re-layouts: 2.75 us -> 0.03 us
    convert_element_type x2 -> x0, other arithmetic: 1.42 us -> none  [the longest x1 0.73 us: shards(): in_use[:, None].astype(jnp.int32)]
    ppermute x8, starting transfers between devices: 17.3 us -> 16.4 us  [the longest x2 10.6 us: across(): gs1 = lax.ppermute(s1, 'azim', az1)]
  transfers between devices with their start and end apart: 8 -> 8, of which waited for: 3 -> 2; matrix products, arithmetic and copies ran while one was open for 0% -> 1% of each run, Pallas kernels for 0% -> 14%
where the time goes in v1:
time: 28.9 us; the launch traced here: 28.8 us
  starting transfers between devices  16.4 us (57%)
  Pallas kernels  9 us (31%)
  waiting for transfers between devices  2.86 us (10%)
    ppermute x2, starting transfers between devices, across(): gs1 = lax.ppermute(s1, 'azim', az1)  10.6 us
    pallas_call x9, Pallas kernels, run(): pl.pallas_call(kernel, out_shape=[jax.ShapeDtypeStruct(s, f32) for s in o...  9 us
    ppermute x2, starting transfers between devices, across(): gr1 = lax.ppermute(r1, ('azim', 'radax'), rad1)  4.2 us
    ppermute x2, waiting for transfers between devices, across(): gr0 = lax.ppermute(r0, 'radax', rad0)  2.59 us
    ppermute x2, starting transfers between devices, across(): gr0 = lax.ppermute(r0, 'radax', rad0)  1.58 us
  transfers between devices with their start and end apart: 8, of which 2 were waited for; matrix products, arithmetic and copies ran while one was open for 1% of the time, Pallas kernels for 14%

profile of v1, /device:TPU:16, one launch (start us, length us, event | category | flops | bytes accessed | tf_op | source)
XLA Modules:
  0.0 28.8 jit_solution(17442632925800191028)
XLA Ops:
  0.0 1.3 %shard_map.58 = (f32[80,128]{1,0:T(8,128)S(1)}, f32[80,128]{1,0:T(8,128)S(1)}) custom-call(f32[8,8,16,320]{3,2,1,0:T(8,128)} %state.1), custom_call_target="tpu_custom_call" | custom-call | bytes 3000000 | tf_op jit(solution)/shard_map/pallas_call | solution.py:440
  1.3 1.6 %collective-permute-start.2 = (f32[80,128]{1,0:T(8,128)S(1)}, f32[80,128]{1,0:T(8,128)S(1)}, u32[]{:S(2)}, u32[]{:S(2)}) collective-permute-start(f32[80,128]{1,0:T(8,128)S(1)} %get-tuple-element.16), channel_id=1, source_target_pairs={{0,1},{1,0},{2,3},{3,2},{4,5},{5,4},{6,7},{7,6},{8,9},{9,8},{10,11... | collective-permute-start | bytes 122888 | tf_op jit(solution)/shard_map/ppermute | solution.py:475
  2.9 1.9 %collective-permute-start.3 = (f32[80,128]{1,0:T(8,128)S(1)}, f32[80,128]{1,0:T(8,128)S(1)}, u32[]{:S(2)}, u32[]{:S(2)}) collective-permute-start(f32[80,128]{1,0:T(8,128)S(1)} %get-tuple-element.17), channel_id=1, source_target_pairs={{0,8},{1,2},{2,1},{3,4},{4,3},{5,6},{6,5},{7,15},{8,0},{9,10},{10,... | collective-permute-start | bytes 122888 | tf_op jit(solution)/shard_map/ppermute | solution.py:473
  4.8 0.0 copy-done.4
  4.8 0.0 copy-done
  4.8 0.0 copy-start.3
  4.8 0.7 %shard_map.55 = (f32[2560,128]{1,0:T(8,128)S(1)}, f32[152,128]{1,0:T(8,128)S(1)}) custom-call(s32[1,2]{1,0:T(1,128)S(1)} %copy-done.1, f32[8,128,320]{2,1,0:T(8,128)S(1)} %bitcast.14, s32[2,3,8]{2,1,0:T(4,128)S(1)} %copy.9.slots), custom_call_target="tpu_custom_call" | custom-call | bytes 3000000 | tf_op jit(solution)/shard_map/pallas_call | solution.py:440
  5.5 6.4 %collective-permute-start.1 = (f32[152,128]{1,0:T(8,128)S(1)}, f32[152,128]{1,0:T(8,128)S(1)}, u32[]{:S(2)}, u32[]{:S(2)}) collective-permute-start(f32[152,128]{1,0:T(8,128)S(1)} %get-tuple-element.15.s1), channel_id=1, source_target_pairs={{0,248},{8,16},{16,8},{24,32},{32,24},{40,48},{48,40},{56,64},{64,... | collective-permute-start | bytes 233480 | tf_op jit(solution)/shard_map/ppermute | solution.py:474
  11.9 0.2 shard_map.57.s0
  12.1 0.0 collective-permute-start
  12.2 0.0 copy-done.3
  12.3 0.0 copy-done.2
  12.3 0.1 mul.13.m
  12.4 0.1 copy.13
  12.5 1.2 %shard_map.56.inner = f32[2560,128]{1,0:T(8,128)S(1)} custom-call(f32[2560,128]{1,0:T(8,128)S(1)} %get-tuple-element.14.q, f32[24,128]{1,0:T(8,128)S(1)} %mul.13.m), custom_call_target="tpu_custom_call" | custom-call | bytes 3000000 | tf_op jit(solution)/shard_map/pallas_call | solution.py:440
  13.7 0.0 collective-permute-done.2.gr0
  13.7 0.0 collective-permute-done.3.gr1
  13.7 0.0 collective-permute-done.ga0
  13.7 0.3 collective-permute-done.1.ga1
  14.0 1.5 %shard_map.59 = (f32[2560,128]{1,0:T(8,128)S(1)}, f32[64,128]{1,0:T(8,128)S(1)}, f32[152,128]{1,0:T(8,128)S(1)}) custom-call(f32[2560,128]{1,0:T(8,128)S(1)} %shard_map.56.inner, f32[2560,128]{1,0:T(8,128)S(1)} %get-tuple-element.14.q, f32[24,128]{1,0:T(8,128)S(1)} %mul.13.m, f32[152,128]{1,0:T(8,128)S(1)} %shard_map.57.s0, ...), custom_call_target="tpu_custom_call" | custom-call | bytes 3000000 | tf_op jit(solution)/shard_map/pallas_call | solution.py:440
  15.5 2.3 %collective-permute-start.7 = (f32[152,128]{1,0:T(8,128)S(1)}, f32[152,128]{1,0:T(8,128)S(1)}, u32[]{:S(2)}, u32[]{:S(2)}) collective-permute-start(f32[152,128]{1,0:T(8,128)S(1)} %get-tuple-element.22), channel_id=1, source_target_pairs={{0,8},{1,2},{2,1},{3,4},{4,3},{5,6},{6,5},{7,15},{8,0},{9,10},{10,... | collective-permute-start | bytes 233480 | tf_op jit(solution)/shard_map/ppermute | solution.py:473
  17.8 0.2 shard_map.62.s1
  18.0 0.4 %shard_map.61 = (f32[144,128]{1,0:T(8,128)S(1)}, f32[80,128]{1,0:T(8,128)S(1)}) custom-call(f32[2560,128]{1,0:T(8,128)S(1)} %get-tuple-element.18.s), custom_call_target="tpu_custom_call" | custom-call | bytes 3000000 | tf_op jit(solution)/shard_map/pallas_call | solution.py:440
  18.4 4.2 %collective-permute-start.5 = (f32[144,128]{1,0:T(8,128)S(1)}, f32[144,128]{1,0:T(8,128)S(1)}, u32[]{:S(2)}, u32[]{:S(2)}) collective-permute-start(f32[144,128]{1,0:T(8,128)S(1)} %shard_map.62.s1), channel_id=1, source_target_pairs={{0,248},{8,16},{16,8},{24,32},{32,24},{40,48},{48,40},{56,64},{64,... | collective-permute-start | bytes 221192 | tf_op jit(solution)/shard_map/ppermute | solution.py:474
  22.6 0.0 collective-permute-start.4
  22.6 0.0 collective-permute-start.6
  22.6 1.4 %shard_map.60.inner = f32[2560,128]{1,0:T(8,128)S(1)} custom-call(f32[2560,128]{1,0:T(8,128)S(1)} %get-tuple-element.18.s, f32[24,128]{1,0:T(8,128)S(1)} %mul.13.m, f32[2560,128]{1,0:T(8,128)S(1)} %get-tuple-element.14.q), custom_call_target="tpu_custom_call" | custom-call | bytes 3000000 | tf_op jit(solution)/shard_map/pallas_call | solution.py:440
  24.0 2.6 %collective-permute-done.6.gr0 = f32[80,128]{1,0:T(8,128)S(1)} collective-permute-done((f32[80,128]{1,0:T(8,128)S(1)}, f32[80,128]{1,0:T(8,128)S(1)}, u32[]{:S(2)}, u32[]{:S(2)}) %collective-permute-start.6) | collective-permute-done | bytes 40992 | tf_op jit(solution)/shard_map/ppermute | solution.py:475
  26.6 0.0 collective-permute-done.5.ga1
  26.6 0.0 collective-permute-done.4.ga0
  26.6 0.0 collective-permute-done.7.gr1
  26.6 2.1 %shard_map.63 = f32[8,128,320]{2,1,0:T(8,128)} custom-call(f32[2560,128]{1,0:T(8,128)S(1)} %shard_map.60.inner, f32[2560,128]{1,0:T(8,128)S(1)} %get-tuple-element.18.s, f32[24,128]{1,0:T(8,128)S(1)} %mul.13.m, f32[144,128]{1,0:T(8,128)S(1)} %get-tuple-element.19.s0, f32[144,128]{1,0:T(8,128)S(1)} %shard_map.62.s1, f32[64,128]{1,0:T(8,128)S(1)} %get-tuple-element.20.matrix, ...), custom_call_target="tpu_custom_call" | custom-call | bytes 3000000 | tf_op jit(solution)/shard_map/pallas_call | solution.py:440
  (14 shorter events, 0.1 us)
Async XLA Ops:
  0.0 4.8 %copy-start = (f32[8,8,16,320]{3,2,1,0:T(8,128)S(1)}, f32[8,8,16,320]{3,2,1,0:T(8,128)}, u32[]{:S(2)}) copy-start(f32[8,8,16,320]{3,2,1,0:T(8,128)} %state.1) | copy-start | bytes 3932164
  0.0 4.8 %copy-start.4 = (s32[1,2,3,8]{3,1,2,0:T(2,128)S(1)}, s32[1,2,3,8]{3,1,2,0:T(2,128)}, u32[]{:S(2)}) copy-start(s32[1,2,3,8]{3,1,2,0:T(2,128)} %param.7) | copy-start | bytes 580
  0.0 4.8 %copy-start.1 = (s32[1,2]{1,0:T(1,128)S(1)}, s32[1,2]{1,0:T(1,128)}, u32[]{:S(2)}) copy-start(s32[1,2]{1,0:T(1,128)} %counts.1) | copy-start | bytes 28
  1.3 12.4 %collective-permute-start.2 = (f32[80,128]{1,0:T(8,128)S(1)}, f32[80,128]{1,0:T(8,128)S(1)}, u32[]{:S(2)}, u32[]{:S(2)}) collective-permute-start(f32[80,128]{1,0:T(8,128)S(1)} %get-tuple-element.16), channel_id=1, source_target_pairs={{0,1},{1,0},{2,3},{3,2},{4,5},{5,4},{6,7},{7,6},{8,9},{9,8},{10,11... | collective-permute-start | bytes 122888 | tf_op jit(solution)/shard_map/ppermute | solution.py:475
  2.9 10.8 %collective-permute-start.3 = (f32[80,128]{1,0:T(8,128)S(1)}, f32[80,128]{1,0:T(8,128)S(1)}, u32[]{:S(2)}, u32[]{:S(2)}) collective-permute-start(f32[80,128]{1,0:T(8,128)S(1)} %get-tuple-element.17), channel_id=1, source_target_pairs={{0,8},{1,2},{2,1},{3,4},{4,3},{5,6},{6,5},{7,15},{8,0},{9,10},{10,... | collective-permute-start | bytes 122888 | tf_op jit(solution)/shard_map/ppermute | solution.py:473
  4.8 7.4 %copy-start.3 = (f32[4,16,4,4]{1,3,2,0:T(4,128)S(1)}, f32[4,16,4,4]{1,3,2,0:T(4,128)}, u32[]{:S(2)}) copy-start(f32[4,16,4,4]{1,3,2,0:T(4,128)} %param.9) | copy-start | bytes 12292
  5.5 6.8 %copy-start.2 = (f32[8,8,16,3]{2,1,3,0:T(8,128)S(1)}, f32[8,8,16,3]{2,1,3,0:T(8,128)}, u32[]{:S(2)}) copy-start(f32[8,8,16,3]{2,1,3,0:T(8,128)} %param.6) | copy-start | bytes 36868
  5.5 8.5 %collective-permute-start.1 = (f32[152,128]{1,0:T(8,128)S(1)}, f32[152,128]{1,0:T(8,128)S(1)}, u32[]{:S(2)}, u32[]{:S(2)}) collective-permute-start(f32[152,128]{1,0:T(8,128)S(1)} %get-tuple-element.15.s1), channel_id=1, source_target_pairs={{0,248},{8,16},{16,8},{24,32},{32,24},{40,48},{48,40},{56,64},{64,... | collective-permute-start | bytes 233480 | tf_op jit(solution)/shard_map/ppermute | solution.py:474
  12.1 1.6 %collective-permute-start = (f32[152,128]{1,0:T(8,128)S(1)}, f32[152,128]{1,0:T(8,128)S(1)}, u32[]{:S(2)}, u32[]{:S(2)}) collective-permute-start(f32[152,128]{1,0:T(8,128)S(1)} %shard_map.57.s0), channel_id=1, source_target_pairs={{0,8},{8,0},{16,24},{24,16},{32,40},{40,32},{48,56},{56,48},{64,72... | collective-permute-start | bytes 233480 | tf_op jit(solution)/shard_map/ppermute | solution.py:476
  15.5 11.1 %collective-permute-start.7 = (f32[152,128]{1,0:T(8,128)S(1)}, f32[152,128]{1,0:T(8,128)S(1)}, u32[]{:S(2)}, u32[]{:S(2)}) collective-permute-start(f32[152,128]{1,0:T(8,128)S(1)} %get-tuple-element.22), channel_id=1, source_target_pairs={{0,8},{1,2},{2,1},{3,4},{4,3},{5,6},{6,5},{7,15},{8,0},{9,10},{10,... | collective-permute-start | bytes 233480 | tf_op jit(solution)/shard_map/ppermute | solution.py:473
  18.4 8.2 %collective-permute-start.5 = (f32[144,128]{1,0:T(8,128)S(1)}, f32[144,128]{1,0:T(8,128)S(1)}, u32[]{:S(2)}, u32[]{:S(2)}) collective-permute-start(f32[144,128]{1,0:T(8,128)S(1)} %shard_map.62.s1), channel_id=1, source_target_pairs={{0,248},{8,16},{16,8},{24,32},{32,24},{40,48},{48,40},{56,64},{64,... | collective-permute-start | bytes 221192 | tf_op jit(solution)/shard_map/ppermute | solution.py:474
  22.6 4.0 %collective-permute-start.4 = (f32[144,128]{1,0:T(8,128)S(1)}, f32[144,128]{1,0:T(8,128)S(1)}, u32[]{:S(2)}, u32[]{:S(2)}) collective-permute-start(f32[144,128]{1,0:T(8,128)S(1)} %get-tuple-element.19.s0), channel_id=1, source_target_pairs={{0,8},{8,0},{16,24},{24,16},{32,40},{40,32},{48,56},{56,48},{64,72... | collective-permute-start | bytes 221192 | tf_op jit(solution)/shard_map/ppermute | solution.py:476
  22.6 4.0 %collective-permute-start.6 = (f32[80,128]{1,0:T(8,128)S(1)}, f32[80,128]{1,0:T(8,128)S(1)}, u32[]{:S(2)}, u32[]{:S(2)}) collective-permute-start(f32[80,128]{1,0:T(8,128)S(1)} %get-tuple-element.21), channel_id=1, source_target_pairs={{0,1},{1,0},{2,3},{3,2},{4,5},{5,4},{6,7},{7,6},{8,9},{9,8},{10,11... | collective-permute-start | bytes 122888 | tf_op jit(solution)/shard_map/ppermute | solution.py:475

commit v2 on v1

--- a/solution.py
+++ b/solution.py
@@ -88,7 +88,7 @@
 
 def position():
     azim, radax = lax.axis_index("azim"), lax.axis_index("radax")
-    return azim & 1, radax & 1, radax
+    return azim & 1, radax & 1, radax, azim
 
 
 def staged(lines, fetch, finish):
@@ -165,16 +165,13 @@
     return 4 if f == 1 + d else 1 + d if f in (0, 4) else None
 
 
-def end_terms(q, m, base, acc, factor, fields, sides):
+def end_terms(q, m, base, acc, factor, fields, sides, directions=(2, 0, 1)):
     for f in fields:
         for i, j in pairs():
             at = pl.ds(row(f, i, j, 1), 16)
             acc[at, :] = base[at, :]
-    for d, nodes in (
-        (2, lambda i, j, k: (i, j, k)),
-        (0, lambda j, k, i: (i, j, k)),
-        (1, lambda i, k, j: (i, j, k)),
-    ):
+    for d in directions:
+        nodes = (lambda j, k, i: (i, j, k), lambda i, k, j: (i, j, k), lambda i, j, k: (i, j, k))[d]
         scale = (3.0 * factor) * m[pl.ds(8 * d, 8), :]
         flow, speed = mean_flow[d], speeds[d]
         old = base if d == 2 else acc
@@ -213,7 +210,7 @@
             message[pl.ds(80 + block * 32 + i * 8, 8), :] = pltpu.roll(packed, side, 1)
 
 
-def pack_blocks(q, side, message):
+def pack_blocks(q, m, side, message):
     place = ((lane_ids() >> 4) + side) & 7
     for g in range(10):
         packed = jnp.zeros((8, 128), f32)
@@ -223,54 +220,73 @@
             at = pl.multiple_of(row(f, i, 0, k) + 96 * side, 8)
             packed = jnp.where(place == p, pltpu.roll(q[pl.ds(at, 8), :], 16 * p, 1), packed)
         message[pl.ds(g * 8, 8), :] = pltpu.roll(packed, 16 * side, 1)
-
-
-def choose(par, ga0, ga1, gr0, gr1, back, ahead, below, above):
-    even = par[0] == 0
-    outward = par[1] == 0
-    rows = back.shape[0]
-    one, two = ga0[pl.ds(0, rows), :], ga1[pl.ds(0, rows), :]
-    back[...] = jnp.where(even, two, one)
-    ahead[...] = jnp.where(even, one, two)
-    one, two = gr0[pl.ds(0, 80), :], gr1[pl.ds(0, 80), :]
-    below[...] = jnp.where(par[2] == 0, 0.0, jnp.where(outward, two, one))
-    above[...] = jnp.where(par[2] == 7, 0.0, jnp.where(outward, one, two))
-
-
-def outside_jumps(back, ahead, below, above, by_rows, mortar):
+    message[pl.ds(80, 8), :] = pltpu.roll(m[pl.ds(8, 8), :], 16 * side, 1)
+
+
+def choose_sectors(par, ga0, ga1, back, ahead):
+    rows = pl.ds(0, back.shape[0])
+    one, two = ga0[rows, :], ga1[rows, :]
+    back[...] = jnp.where(par[0] == 0, two, one)
+    ahead[...] = jnp.where(par[0] == 0, one, two)
+
+
+def choose_blocks(par, gr0, gr1, below, above):
+    rows = pl.ds(0, below.shape[0])
+    one, two = gr0[rows, :], gr1[rows, :]
+    below[...] = jnp.where(par[2] == 0, 0.0, jnp.where(par[1] == 0, two, one))
+    above[...] = jnp.where(par[2] == 7, 0.0, jnp.where(par[1] == 0, one, two))
+
+
+def sector_jumps(back, ahead, mortar):
     sub = lax.broadcasted_iota(jnp.int32, (8, 128), 0)
-    lanes = lane_ids()
-    axial = lanes & 15
+    axial = lane_ids() & 15
 
     def az(f, j, k, x0, x3):
         at = pl.ds(f * 16 + 4 * j + k, 1)
         return jnp.where(sub == 0, back[at, :] - x0, 0.0), jnp.where(sub == 7, ahead[at, :] - x3, 0.0)
 
-    def rad(f, i, k, x0, x3):
-        n = f * 16 + 4 * i + k
-        if by_rows:
-            at = pl.ds(n, 1)
-            before = pltpu.roll(jnp.broadcast_to(below[at, :], (8, 128)), 16, 1, stride=16, stride_axis=0)
-            after = pltpu.roll(jnp.broadcast_to(above[at, :], (8, 128)), 0, 1, stride=16, stride_axis=0)
-        else:
-            g, p = divmod(n, 8)
-            at = pl.ds(g * 8, 8)
-            before = pltpu.roll(below[at, :], (128 - 16 * p) % 128, 1)
-            after = pltpu.roll(above[at, :], (112 - 16 * p) % 128, 1)
-        return jnp.where(lanes < 16, before - x0, 0.0), jnp.where(lanes >= 112, after - x3, 0.0)
-
     def ax(f, i, j, x0, x3):
         to_stator, to_rotor = mortar(f, i, j)
         return jnp.where(axial == 8, to_stator, 0.0), jnp.where(axial == 7, to_rotor, 0.0)
 
-    return {0: az, 1: rad, 2: ax}
+    return {0: az, 2: ax}
+
+
+def rim_jumps(below, above):
+    lanes = lane_ids()
+
+    def rad(f, i, k, x0, x3):
+        at = pl.ds(f * 16 + 4 * i + k, 1)
+        before = pltpu.roll(jnp.broadcast_to(below[at, :], (8, 128)), 16, 1, stride=16, stride_axis=0)
+        after = pltpu.roll(jnp.broadcast_to(above[at, :], (8, 128)), 0, 1, stride=16, stride_axis=0)
+        return jnp.where(lanes < 16, before - x0, 0.0), jnp.where(lanes >= 112, after - x3, 0.0)
+
+    return rad
+
+
+def block_jumps(below, above, owed):
+    lanes = lane_ids()
+    m_below = below[pl.ds(80, 8), :]
+    m_above = pltpu.roll(above[pl.ds(80, 8), :], 112, 1)
+
+    def rad(f, i, k, x0, x3):
+        n = f * 16 + 4 * i + k
+        g, p = divmod(n, 8)
+        at = pl.ds(g * 8, 8)
+        before = pltpu.roll(below[at, :], (128 - 16 * p) % 128, 1) + m_below * owed[pl.ds(n * 16, 8), :]
+        after = pltpu.roll(above[at, :], (112 - 16 * p) % 128, 1) + m_above * owed[pl.ds(n * 16 + 8, 8), :]
+        return jnp.where(lanes < 16, before - x0, 0.0), jnp.where(lanes >= 112, after - x3, 0.0)
+
+    return rad
 
 
 def mortar_matrix(lists, following, tables):
     own, later = lists.T, following.T
 
     def column(t):
-        return jnp.concatenate([own[0:8, t : t + 1], own[0:8, t + 3 : t + 4], later[0:8, t : t + 1]], axis=0)
+        return jnp.concatenate(
+            [own[0:8, 2 * t : 2 * t + 1], own[0:8, 2 * t + 1 : 2 * t + 2], later[0:8, 2 * t : 2 * t + 1]], axis=0
+        )
 
     rotor, stator, kind = (column(t) for t in range(3))
     slot = lax.broadcasted_iota(jnp.int32, (24, 1), 0)
@@ -330,75 +346,119 @@
     return mortar
 
 
-def rim_kernel(state, r0, r1, rims, sems):
-    par = position()
-    copies = [pltpu.make_async_copy(state.at[:, 7 * e], rims.at[e], sems.at[e]) for e in range(2)]
+def rim_rows(pieces, side, message):
+    for c in (0, 128, 256):
+        width = min(128, 320 - c)
+        block = jnp.concatenate([pieces(7 - a, c, width) for a in range(8)], axis=0).T
+        for g in range(width // 16):
+            at = 16 * g
+            chosen = jnp.where(side == 0, block[at : at + 4], block[at + 12 : at + 16])
+            message[pl.ds(c // 4 + 4 * g, 4), :] = chosen
+
+
+def rim_message(nat, side, message):
+    start = pl.multiple_of(112 * side, 16)
+    rim_rows(lambda a, c, width: nat[a, pl.ds(start, 16), c : c + width], side, message)
+
+
+def enter_kernel(state, nat, q, sems):
+    copies = [pltpu.make_async_copy(state.at[a], nat.at[a], sems.at[a]) for a in range(8)]
     for copy in copies:
         copy.start()
-    for e in range(2):
-        copies[e].wait()
-    even = par[1] == 0
-    for c in (0, 128, 256):
-        width = min(128, 320 - c)
-        low, high = (
-            jnp.concatenate([rims[e, 7 - a, :, c : c + width] for a in range(8)], axis=0).T for e in range(2)
-        )
-        for g in range(width // 16):
-            at = 16 * g
-            down, up = low[at : at + 4], high[at + 12 : at + 16]
-            r1[pl.ds(c // 4 + 4 * g, 4), :] = jnp.where(even, down, up)
-            r0[pl.ds(c // 4 + 4 * g, 4), :] = jnp.where(even, up, down)
-
-
-def enter_kernel(counts, nat, slots, q, s1):
-    par = position()
     for a in range(8):
+        copies[a].wait()
         for c in (0, 128, 256):
             width = min(128, 320 - c)
             q[pl.ds(c * 8 + a, width, stride=8), :] = nat[a, :, c : c + width].T
-    pack_sector(q, par[0], s1)
-    lists = jnp.concatenate(
-        [
-            jnp.concatenate([slots[b].astype(f32) for b in range(2)], axis=0),
-            jnp.concatenate(
-                [jnp.broadcast_to(counts[:, b : b + 1].astype(f32), (1, 8)) for b in range(2)], axis=0
-            ),
-        ],
-        axis=0,
-    )
+
+
+def first_kernel(counts, q, slots, inner, s1):
+    pack_sector(q, position()[0], s1)
+    used = jnp.concatenate(
+        [jnp.broadcast_to(counts[:, b : b + 1].astype(f32), (1, 8)) for b in range(2)], axis=0
+    )
+    lists = jnp.concatenate([slots[t].astype(f32) for t in range(3)] + [used], axis=0)
     s1[pl.ds(144, 8), :] = jnp.concatenate([lists, jnp.zeros((8, 120), f32)], axis=1)
 
 
-def others_kernel(q, s1, s0):
+def rim_kernel(nat, s1, r1):
+    rim_message(nat, position()[1], r1)
+
+
+def others_kernel(nat, q, s1, r1, s0, r0):
     par = position()
+    rim_message(nat, 1 - par[1], r0)
     pack_sector(q, 1 - par[0], s0)
     s0[pl.ds(144, 8), :] = s1[pl.ds(144, 8), :]
 
 
-def inner_kernel(q, m, acc):
-    inner_operator(q, m, acc, lambda x, *at: x)
-
-
-def middle_kernel(
-    inner, q, m, s0, s1, tables, ga0, ga1, gr0, gr1, s, matrix, r1, placed, back, ahead, below, above
-):
+def ahead_kernel(q, m, counts, slots, acc):
+    @pl.when(position()[3] < 16)
+    def _():
+        inner_operator(q, m, acc, lambda x, *at: x)
+
+
+def inner_kernel(q, m, early, acc):
+    before = position()[3] < 16
+
+    @pl.when(before)
+    def _():
+        acc[...] = early[...]
+
+    @pl.when(jnp.logical_not(before))
+    def _():
+        inner_operator(q, m, acc, lambda x, *at: x)
+
+
+def middle_kernel(inner, q, m, s0, s1, tables, ga0, ga1, part, matrix, r1, placed, back, ahead):
     par = position()
-    choose(par, ga0, ga1, gr0, gr1, back, ahead, below, above)
+    choose_sectors(par, ga0, ga1, back, ahead)
     matrix[...] = mortar_matrix(s1[pl.ds(144, 8), :], ahead[pl.ds(144, 8), :], tables[...])
     mortar = mortar_terms(par, matrix[...], s0, s1, back, ahead, placed)
-    end_terms(q, m, inner, s, 1.0, range(5), outside_jumps(back, ahead, below, above, True, mortar))
-    pack_blocks(s, par[1], r1)
-    r1[pl.ds(80, 72), :] = jnp.zeros((72, 128), f32)
+    end_terms(q, m, inner, part, 1.0, range(5), sector_jumps(back, ahead, mortar), (2, 0))
+    pack_blocks(part, m, par[1], r1)
+    pad = r1.shape[0] - 88
+    if pad:
+        r1[pl.ds(88, pad), :] = jnp.zeros((pad, 128), f32)
+
+
+def block_kernel(part, q, m, gr0, gr1, s, owed, below, above):
+    choose_blocks(position(), gr0, gr1, below, above)
+    rad = rim_jumps(below, above)
+    scale = 3.0 * m[pl.ds(8, 8), :]
+    for f in range(5):
+        for i in range(4):
+            at = pl.ds(row(f, i, 1, 0), 64)
+            s[at, :] = part[at, :]
+
+    def fetch(i, k):
+        return ([rad(f, i, k, tile(q, f, i, 0, k), tile(q, f, i, 3, k)) for f in range(5)],)
+
+    def finish(i, k, jumps):
+        for f in range(5):
+            other = coupled(f, 1)
+            low, high = jumps[f]
+            lower, upper = (low, high) if other is None else (low + jumps[other][0], high - jumps[other][1])
+            theirs, yours = (low, high) if other is None else (low - jumps[other][0], high + jumps[other][1])
+            for j, term in ((0, lower), (3, upper)):
+                at = pl.ds(row(f, i, j, k), 8)
+                s[at, :] = part[at, :] + scale * term
+            n = f * 16 + 4 * i + k
+            owed[pl.ds(n * 16, 8), :] = -3.0 * theirs
+            owed[pl.ds(n * 16 + 8, 8), :] = -3.0 * yours
+
+    staged(pairs(), fetch, finish)
 
 
 def sector_kernel(s, s1):
     par = position()
     pack_sector(s, par[0], s1)
-
-
-def later_kernel(s, s0, r0):
+    s1[pl.ds(144, 8), :] = jnp.zeros((8, 128), f32)
+
+
+def later_kernel(s, part, m, s0, r0):
     par = position()
-    pack_blocks(s, 1 - par[1], r0)
+    pack_blocks(part, m, 1 - par[1], r0)
     pack_sector(s, 1 - par[0], s0)
 
 
@@ -413,12 +473,14 @@
 
 
 def last_kernel(
-    inner, s, m, s0, s1, matrix, ga0, ga1, gr0, gr1, out, acc, placed, back, ahead, below, above, turned, sems
+    inner, s, m, s0, s1, matrix, owed, ga0, ga1, gr0, gr1, out, acc, placed, back, ahead, below, above, turned, sems
 ):
     par = position()
-    choose(par, ga0, ga1, gr0, gr1, back, ahead, below, above)
+    choose_sectors(par, ga0, ga1, back, ahead)
+    choose_blocks(par, gr0, gr1, below, above)
     mortar = mortar_terms(par, matrix[...], s0, s1, back, ahead, placed)
-    jumps = outside_jumps(back, ahead, below, above, False, mortar)
+    jumps = sector_jumps(back, ahead, mortar)
+    jumps[1] = block_jumps(below, above, owed)
     copies = []
     for c, fields in ((128, (2, 3)), (0, (0, 1)), (256, (4,))):
         width = min(128, 320 - c)
@@ -478,27 +540,31 @@
 
     state, rim, trace, first_trace = (2560, 128), (80, 128), (144, 128), (152, 128)
     dma = pltpu.SemaphoreType.DMA
-    r0, r1 = call(rim_kernel, [rim, rim], [(2, 8, 16, 320), dma((2,))], {0: pltpu.HBM}, limit=53)(solution)
     turned = jnp.concatenate([projections[:2], projections[2:].transpose(0, 1, 3, 2)], axis=0)
     tables = jnp.repeat(turned.transpose(1, 0, 2, 3).reshape(16, 64), 8, axis=1)
     tables = jnp.pad(tables, ((0, 112), (0, 0)))
     m = time_step * metric.transpose(3, 0, 1, 2).reshape(24, 128)
-    nat = solution.reshape(8, 128, 320)
-    q, s1 = call(enter_kernel, [state, first_trace])(counts, nat, intersections[0])
-    (s0,) = call(others_kernel, [first_trace])(q, s1)
-    got = across(r0, r1, s0, s1)
-    (inner,) = call(inner_kernel, [state])(q, m)
-    sides = [(64, 256), first_trace, first_trace, rim, rim]
-    s, matrix, r1 = call(middle_kernel, [state, (64, 128), first_trace], sides)(
-        inner, q, m, s0, s1, tables, *got
-    )
-    (s1,) = call(sector_kernel, [trace])(s)
-    s0, r0 = call(later_kernel, [trace, rim])(s)
+    nat, q = call(enter_kernel, [(8, 128, 320), state], [dma((8,))], {0: pltpu.HBM}, limit=50)(
+        solution.reshape(8, 128, 320)
+    )
+    slots = intersections.transpose(0, 2, 1, 3)[0]
+    (early,) = call(ahead_kernel, [state])(q, m, counts, slots)
+    (s1,) = call(first_kernel, [first_trace])(counts, q, slots, early)
+    (r1,) = call(rim_kernel, [rim])(nat, s1)
+    s0, r0 = call(others_kernel, [first_trace, rim])(nat, q, s1, r1)
+    ga0, ga1, gr0, gr1 = across(r0, r1, s0, s1)
+    (inner,) = call(inner_kernel, [state])(q, m, early)
+    part, matrix, r1 = call(
+        middle_kernel, [state, (64, 128), (160, 128)], [(64, 256), first_trace, first_trace]
+    )(inner, q, m, s0, s1, tables, ga0, ga1)
+    s, owed = call(block_kernel, [state, (1280, 128)], [rim, rim])(part, q, m, gr0, gr1)
+    (s1,) = call(sector_kernel, [first_trace])(s)
+    s0, r0 = call(later_kernel, [trace, (88, 128)])(s, part, m)
     got = across(r0, r1, s0, s1)
     (inner,) = call(inner_last_kernel, [state])(s, m, q)
-    sides = [state, (64, 256), trace, trace, rim, rim]
+    sides = [state, (64, 256), trace, trace, (88, 128), (88, 128)]
     (out,) = call(last_kernel, [(8, 128, 320)], sides + [(8, 128, 320), dma((24,))], {}, pltpu.HBM)(
-        inner, s, m, s0, s1, matrix, *got
+        inner, s, m, s0, s1, matrix, owed, *got
     )
     return out.reshape(solution.shape)
 

time: 28.9 us -> 26.8 us (0.927)
  starting transfers between devices: 16.4 us -> 13 us
  Pallas kernels: 9 us -> 9.76 us
  waiting for transfers between devices: 2.86 us -> 3.33 us
    ppermute x2, starting transfers between devices: 10.6 us -> 6.57 us  [across(): gs1 = lax.ppermute(s1, 'azim', az1)]
    ppermute x2, starting transfers between devices: 4.2 us -> 5.79 us  [across(): gr1 = lax.ppermute(r1, ('azim', 'radax'), rad1)]
    ppermute x2, starting transfers between devices: 1.58 us -> 0.52 us  [across(): gr0 = lax.ppermute(r0, 'radax', rad0)]
    pallas_call x9 -> x12, Pallas kernels: 9 us -> 9.76 us  [run(): pl.pallas_call(kernel, out_shape=[jax.ShapeDtypeStruct(s, f32) for s in o...]
    ppermute x2, waiting for transfers between devices: 0.01 us -> 0.69 us  [across(): gs0 = lax.ppermute(s0, 'azim', az0)]
  transfers between devices with their start and end apart: 8 -> 8, of which waited for: 2 -> 2; matrix products, arithmetic and copies ran while one was open for 1% -> 1% of each run, Pallas kernels for 14% -> 16%
where the time goes in v2:
time: 26.8 us; the launch traced here: 26.7 us
  starting transfers between devices  13 us (49%)
  Pallas kernels  9.76 us (36%)
  waiting for transfers between devices  3.33 us (12%)
  between operations  0.33 us (1%)
  local copies, waits for them, and re-layouts  0.28 us (1%)
    pallas_call x12, Pallas kernels, run(): pl.pallas_call(kernel, out_shape=[jax.ShapeDtypeStruct(s, f32) for s in o...  9.76 us
    ppermute x2, starting transfers between devices, across(): gs1 = lax.ppermute(s1, 'azim', az1)  6.57 us
    ppermute x2, starting transfers between devices, across(): gr1 = lax.ppermute(r1, ('azim', 'radax'), rad1)  5.79 us
    ppermute x2, waiting for transfers between devices, across(): gr0 = lax.ppermute(r0, 'radax', rad0)  2.63 us
    ppermute x2, waiting for transfers between devices, across(): gs0 = lax.ppermute(s0, 'azim', az0)  0.69 us
  transfers between devices with their start and end apart: 8, of which 2 were waited for; matrix products, arithmetic and copies ran while one was open for 1% of the time, Pallas kernels for 16%

profile of v2, /device:TPU:16, one launch (start us, length us, event | category | flops | bytes accessed | tf_op | source)
XLA Modules:
  0.0 26.7 jit_solution(13192199752997926464)
XLA Ops:
  0.0 2.0 %shard_map.55 = (f32[8,128,320]{2,1,0:T(8,128)S(1)}, f32[2560,128]{1,0:T(8,128)S(1)}) custom-call(f32[8,128,320]{2,1,0:T(8,128)} %bitcast.18), custom_call_target="tpu_custom_call" | custom-call | bytes 3000000 | tf_op jit(solution)/shard_map/pallas_call | solution.py:502
  2.0 0.0 copy-done.2
  2.0 0.1 mul.13.m
  2.2 1.2 %shard_map.56.early.inner = f32[2560,128]{1,0:T(8,128)S(1)} custom-call(f32[2560,128]{1,0:T(8,128)S(1)} %get-tuple-element.16.q, f32[24,128]{1,0:T(8,128)S(1)} %mul.13.m, s32[1,2]{1,0:T(1,128)S(1)} %copy-done.1, s32[3,2,8]{2,1,0:T(2,128)S(1)} %bitcast.16), custom_call_target="tpu_custom_call" | custom-call | bytes 3000000 | tf_op jit(solution)/shard_map/pallas_call | solution.py:502
  3.3 0.2 shard_map.58.s1
  3.6 4.9 %collective-permute-start.1 = (f32[152,128]{1,0:T(8,128)S(1)}, f32[152,128]{1,0:T(8,128)S(1)}, u32[]{:S(2)}, u32[]{:S(2)}) collective-permute-start(f32[152,128]{1,0:T(8,128)S(1)} %shard_map.58.s1), channel_id=1, source_target_pairs={{0,248},{8,16},{16,8},{24,32},{32,24},{40,48},{48,40},{56,64},{64,... | collective-permute-start | bytes 233480 | tf_op jit(solution)/shard_map/ppermute | solution.py:536
  8.5 0.1 shard_map.59.r1
  8.6 0.0 copy-start.3
  8.6 2.9 %collective-permute-start.3 = (f32[80,128]{1,0:T(8,128)S(1)}, f32[80,128]{1,0:T(8,128)S(1)}, u32[]{:S(2)}, u32[]{:S(2)}) collective-permute-start(f32[80,128]{1,0:T(8,128)S(1)} %shard_map.59.r1), channel_id=1, source_target_pairs={{0,8},{1,2},{2,1},{3,4},{4,3},{5,6},{6,5},{7,15},{8,0},{9,10},{10,... | collective-permute-start | bytes 122888 | tf_op jit(solution)/shard_map/ppermute | solution.py:535
  11.5 0.3 %shard_map.60 = (f32[152,128]{1,0:T(8,128)S(1)}, f32[80,128]{1,0:T(8,128)S(1)}) custom-call(f32[8,128,320]{2,1,0:T(8,128)S(1)} %get-tuple-element.17.nat, f32[2560,128]{1,0:T(8,128)S(1)} %get-tuple-element.16.q, f32[152,128]{1,0:T(8,128)S(1)} %shard_map.58.s1, f32[80,128]{1,0:T(8,128)S(1)} %shard_map.59.r1), custom_call_target="tpu_custom_call" | custom-call | bytes 3000000 | tf_op jit(solution)/shard_map/pallas_call | solution.py:502
  11.8 0.0 collective-permute-start
  11.8 0.2 collective-permute-start.2
  12.1 0.1 shard_map.57.inner
  12.3 0.1 copy.11
  12.4 0.7 %collective-permute-done.ga0 = f32[152,128]{1,0:T(8,128)S(1)} collective-permute-done((f32[152,128]{1,0:T(8,128)S(1)}, f32[152,128]{1,0:T(8,128)S(1)}, u32[]{:S(2)}, u32[]{:S(2)}) %collective-permute-start) | collective-permute-done | bytes 77856 | tf_op jit(solution)/shard_map/ppermute | solution.py:538
  13.1 0.0 collective-permute-done.1.ga1
  13.1 1.5 %shard_map.61 = (f32[2560,128]{1,0:T(8,128)S(1)}, f32[64,128]{1,0:T(8,128)S(1)}, f32[160,128]{1,0:T(8,128)S(1)}) custom-call(f32[2560,128]{1,0:T(8,128)S(1)} %shard_map.57.inner, f32[2560,128]{1,0:T(8,128)S(1)} %get-tuple-element.16.q, f32[24,128]{1,0:T(8,128)S(1)} %mul.13.m, f32[152,128]{1,0:T(8,128)S(1)} %get-tuple-element.18.s0, ...), custom_call_target="tpu_custom_call" | custom-call | bytes 3000000 | tf_op jit(solution)/shard_map/pallas_call | solution.py:502
  14.5 2.9 %collective-permute-start.7 = (f32[160,128]{1,0:T(8,128)S(1)}, f32[160,128]{1,0:T(8,128)S(1)}, u32[]{:S(2)}, u32[]{:S(2)}) collective-permute-start(f32[160,128]{1,0:T(8,128)S(1)} %get-tuple-element.26), channel_id=1, source_target_pairs={{0,8},{1,2},{2,1},{3,4},{4,3},{5,6},{6,5},{7,15},{8,0},{9,10},{10,... | collective-permute-start | bytes 245768 | tf_op jit(solution)/shard_map/ppermute | solution.py:535
  17.4 0.0 collective-permute-done.2.gr0
  17.4 0.0 collective-permute-done.3.gr1
  17.4 0.3 %shard_map.62 = (f32[2560,128]{1,0:T(8,128)S(1)}, f32[1280,128]{1,0:T(8,128)S(1)}) custom-call(f32[2560,128]{1,0:T(8,128)S(1)} %get-tuple-element.19.part, f32[2560,128]{1,0:T(8,128)S(1)} %get-tuple-element.16.q, f32[24,128]{1,0:T(8,128)S(1)} %mul.13.m, f32[80,128]{1,0:T(8,128)S(1)} %collective-permute-done.2.gr0, f32[80,128]{1,0:T(8,128)S(1)} %collective-permute-done.3.gr1), custom_call_target="tpu_custom_call" | custom-call | bytes 3000000 | tf_op jit(solution)/shard_map/pallas_call | solution.py:502
  17.7 0.2 shard_map.65.s1
  17.9 1.7 %collective-permute-start.5 = (f32[152,128]{1,0:T(8,128)S(1)}, f32[152,128]{1,0:T(8,128)S(1)}, u32[]{:S(2)}, u32[]{:S(2)}) collective-permute-start(f32[152,128]{1,0:T(8,128)S(1)} %shard_map.65.s1), channel_id=1, source_target_pairs={{0,248},{8,16},{16,8},{24,32},{32,24},{40,48},{48,40},{56,64},{64,... | collective-permute-start | bytes 233480 | tf_op jit(solution)/shard_map/ppermute | solution.py:536
  19.6 0.4 %shard_map.64 = (f32[144,128]{1,0:T(8,128)S(1)}, f32[88,128]{1,0:T(8,128)S(1)}) custom-call(f32[2560,128]{1,0:T(8,128)S(1)} %get-tuple-element.21.s, f32[2560,128]{1,0:T(8,128)S(1)} %get-tuple-element.19.part, f32[24,128]{1,0:T(8,128)S(1)} %mul.13.m), custom_call_target="tpu_custom_call" | custom-call | bytes 3000000 | tf_op jit(solution)/shard_map/pallas_call | solution.py:502
  20.0 0.0 collective-permute-start.4
  20.0 0.3 %collective-permute-start.6 = (f32[88,128]{1,0:T(8,128)S(1)}, f32[88,128]{1,0:T(8,128)S(1)}, u32[]{:S(2)}, u32[]{:S(2)}) collective-permute-start(f32[88,128]{1,0:T(8,128)S(1)} %get-tuple-element.25), channel_id=1, source_target_pairs={{0,1},{1,0},{2,3},{3,2},{4,5},{5,4},{6,7},{7,6},{8,9},{9,8},{10,11... | collective-permute-start | bytes 135176 | tf_op jit(solution)/shard_map/ppermute | solution.py:537
  20.3 1.4 %shard_map.63.inner = f32[2560,128]{1,0:T(8,128)S(1)} custom-call(f32[2560,128]{1,0:T(8,128)S(1)} %get-tuple-element.21.s, f32[24,128]{1,0:T(8,128)S(1)} %mul.13.m, f32[2560,128]{1,0:T(8,128)S(1)} %get-tuple-element.16.q), custom_call_target="tpu_custom_call" | custom-call | bytes 3000000 | tf_op jit(solution)/shard_map/pallas_call | solution.py:502
  21.7 2.6 %collective-permute-done.6.gr0 = f32[88,128]{1,0:T(8,128)S(1)} collective-permute-done((f32[88,128]{1,0:T(8,128)S(1)}, f32[88,128]{1,0:T(8,128)S(1)}, u32[]{:S(2)}, u32[]{:S(2)}) %collective-permute-start.6) | collective-permute-done | bytes 45088 | tf_op jit(solution)/shard_map/ppermute | solution.py:537
  24.3 0.0 collective-permute-done.4.ga0
  24.3 0.0 collective-permute-done.5.ga1
  24.3 0.0 collective-permute-done.7.gr1
  24.4 2.2 %shard_map.66 = f32[8,128,320]{2,1,0:T(8,128)} custom-call(f32[2560,128]{1,0:T(8,128)S(1)} %shard_map.63.inner, f32[2560,128]{1,0:T(8,128)S(1)} %get-tuple-element.21.s, f32[24,128]{1,0:T(8,128)S(1)} %mul.13.m, f32[144,128]{1,0:T(8,128)S(1)} %get-tuple-element.22.s0, f32[152,128]{1,0:T(8,128)S(1)} %shard_map.65.s1, f32[64,128]{1,0:T(8,128)S(1)} %get-tuple-element.23.matrix, ...), custom_call_target="tpu_custom_call" | custom-call | bytes 3000000 | tf_op jit(solution)/shard_map/pallas_call | solution.py:502
  (14 shorter events, 0.1 us)
Async XLA Ops:
  0.0 2.0 %copy-start.2 = (f32[8,8,16,3]{2,1,3,0:T(8,128)S(1)}, f32[8,8,16,3]{2,1,3,0:T(8,128)}, u32[]{:S(2)}) copy-start(f32[8,8,16,3]{2,1,3,0:T(8,128)} %param.6) | copy-start | bytes 36868
  0.0 2.1 %copy-start = (s32[1,2,3,8]{3,1,2,0:T(2,128)S(1)}, s32[1,2,3,8]{3,1,2,0:T(2,128)}, u32[]{:S(2)}) copy-start(s32[1,2,3,8]{3,1,2,0:T(2,128)} %param.7) | copy-start | bytes 580
  0.0 2.1 %copy-start.1 = (s32[1,2]{1,0:T(1,128)S(1)}, s32[1,2]{1,0:T(1,128)}, u32[]{:S(2)}) copy-start(s32[1,2]{1,0:T(1,128)} %counts.3) | copy-start | bytes 28
  3.6 9.5 %collective-permute-start.1 = (f32[152,128]{1,0:T(8,128)S(1)}, f32[152,128]{1,0:T(8,128)S(1)}, u32[]{:S(2)}, u32[]{:S(2)}) collective-permute-start(f32[152,128]{1,0:T(8,128)S(1)} %shard_map.58.s1), channel_id=1, source_target_pairs={{0,248},{8,16},{16,8},{24,32},{32,24},{40,48},{48,40},{56,64},{64,... | collective-permute-start | bytes 233480 | tf_op jit(solution)/shard_map/ppermute | solution.py:536
  8.6 3.5 %copy-start.3 = (f32[4,16,4,4]{1,3,2,0:T(4,128)S(1)}, f32[4,16,4,4]{1,3,2,0:T(4,128)}, u32[]{:S(2)}) copy-start(f32[4,16,4,4]{1,3,2,0:T(4,128)} %param.9) | copy-start | bytes 12292
  8.6 8.8 %collective-permute-start.3 = (f32[80,128]{1,0:T(8,128)S(1)}, f32[80,128]{1,0:T(8,128)S(1)}, u32[]{:S(2)}, u32[]{:S(2)}) collective-permute-start(f32[80,128]{1,0:T(8,128)S(1)} %shard_map.59.r1), channel_id=1, source_target_pairs={{0,8},{1,2},{2,1},{3,4},{4,3},{5,6},{6,5},{7,15},{8,0},{9,10},{10,... | collective-permute-start | bytes 122888 | tf_op jit(solution)/shard_map/ppermute | solution.py:535
  11.8 1.3 %collective-permute-start = (f32[152,128]{1,0:T(8,128)S(1)}, f32[152,128]{1,0:T(8,128)S(1)}, u32[]{:S(2)}, u32[]{:S(2)}) collective-permute-start(f32[152,128]{1,0:T(8,128)S(1)} %get-tuple-element.18.s0), channel_id=1, source_target_pairs={{0,8},{8,0},{16,24},{24,16},{32,40},{40,32},{48,56},{56,48},{64,72... | collective-permute-start | bytes 233480 | tf_op jit(solution)/shard_map/ppermute | solution.py:538
  11.8 5.6 %collective-permute-start.2 = (f32[80,128]{1,0:T(8,128)S(1)}, f32[80,128]{1,0:T(8,128)S(1)}, u32[]{:S(2)}, u32[]{:S(2)}) collective-permute-start(f32[80,128]{1,0:T(8,128)S(1)} %get-tuple-element.20), channel_id=1, source_target_pairs={{0,1},{1,0},{2,3},{3,2},{4,5},{5,4},{6,7},{7,6},{8,9},{9,8},{10,11... | collective-permute-start | bytes 122888 | tf_op jit(solution)/shard_map/ppermute | solution.py:537
  14.5 9.8 %collective-permute-start.7 = (f32[160,128]{1,0:T(8,128)S(1)}, f32[160,128]{1,0:T(8,128)S(1)}, u32[]{:S(2)}, u32[]{:S(2)}) collective-permute-start(f32[160,128]{1,0:T(8,128)S(1)} %get-tuple-element.26), channel_id=1, source_target_pairs={{0,8},{1,2},{2,1},{3,4},{4,3},{5,6},{6,5},{7,15},{8,0},{9,10},{10,... | collective-permute-start | bytes 245768 | tf_op jit(solution)/shard_map/ppermute | solution.py:535
  17.9 6.4 %collective-permute-start.5 = (f32[152,128]{1,0:T(8,128)S(1)}, f32[152,128]{1,0:T(8,128)S(1)}, u32[]{:S(2)}, u32[]{:S(2)}) collective-permute-start(f32[152,128]{1,0:T(8,128)S(1)} %shard_map.65.s1), channel_id=1, source_target_pairs={{0,248},{8,16},{16,8},{24,32},{32,24},{40,48},{48,40},{56,64},{64,... | collective-permute-start | bytes 233480 | tf_op jit(solution)/shard_map/ppermute | solution.py:536
  20.0 4.4 %collective-permute-start.4 = (f32[144,128]{1,0:T(8,128)S(1)}, f32[144,128]{1,0:T(8,128)S(1)}, u32[]{:S(2)}, u32[]{:S(2)}) collective-permute-start(f32[144,128]{1,0:T(8,128)S(1)} %get-tuple-element.22.s0), channel_id=1, source_target_pairs={{0,8},{8,0},{16,24},{24,16},{32,40},{40,32},{48,56},{56,48},{64,72... | collective-permute-start | bytes 221192 | tf_op jit(solution)/shard_map/ppermute | solution.py:538
  20.0 4.3 %collective-permute-start.6 = (f32[88,128]{1,0:T(8,128)S(1)}, f32[88,128]{1,0:T(8,128)S(1)}, u32[]{:S(2)}, u32[]{:S(2)}) collective-permute-start(f32[88,128]{1,0:T(8,128)S(1)} %get-tuple-element.25), channel_id=1, source_target_pairs={{0,1},{1,0},{2,3},{3,2},{4,5},{5,4},{6,7},{7,6},{8,9},{9,8},{10,11... | collective-permute-start | bytes 135176 | tf_op jit(solution)/shard_map/ppermute | solution.py:537

commit v3 on v2

--- a/solution.py
+++ b/solution.py
@@ -199,15 +199,13 @@
         low = q[pl.ds(f * 64 * 8, 16, stride=8), :]
         high = q[pl.ds((f * 64 + 48) * 8 + 7, 16, stride=8), :]
         message[pl.ds(f * 16, 16), :] = jnp.where(side == 0, low, high)
-    for i in range(4):
-        for block, fields in ((0, range(4)), (1, (4,))):
-            packed = jnp.zeros((8, 128), f32)
-            for f in fields:
-                for j in range(4):
-                    p = 4 * (f % 4) + j
-                    at = pl.multiple_of(row(f, i, j, 0) + 24 * side, 8)
-                    packed = jnp.where(spot == p, pltpu.roll(q[pl.ds(at, 8), :], (120 + p) % 128, 1), packed)
-            message[pl.ds(80 + block * 32 + i * 8, 8), :] = pltpu.roll(packed, side, 1)
+    for group in range(5):
+        packed = jnp.zeros((8, 128), f32)
+        for p in range(16):
+            f, i, j = (p // 4, group, p % 4) if group < 4 else (4, p // 4, p % 4)
+            at = pl.multiple_of(row(f, i, j, 0) + 24 * side, 8)
+            packed = jnp.where(spot == p, pltpu.roll(q[pl.ds(at, 8), :], (120 + p) % 128, 1), packed)
+        message[pl.ds(80 + group * 8, 8), :] = pltpu.roll(packed, side, 1)
 
 
 def pack_blocks(q, m, side, message):
@@ -327,12 +325,19 @@
 
 def mortar_terms(par, matrix, s0, s1, back, ahead, placed):
     even = par[0] == 0
+
+    def four(ref):
+        return ref[pl.ds(80, 32), :]
+
+    def fifth(ref):
+        packed = ref[pl.ds(112, 8), :]
+        return jnp.concatenate([packed] + [pltpu.roll(packed, 128 - 4 * i, 1) for i in range(1, 4)], axis=0)
+
     blocks = []
-    for block in range(2):
-        at = pl.ds(80 + block * 32, 32)
-        one, two = s0[at, :], s1[at, :]
+    for part in (four, fifth):
+        one, two = part(s0), part(s1)
         mine, yours = jnp.where(even, one, two), jnp.where(even, two, one)
-        blocks.append(jnp.concatenate([back[at, :], mine, yours, ahead[at, :]], axis=0))
+        blocks.append(jnp.concatenate([part(back), mine, yours, part(ahead)], axis=0))
     traces = jnp.concatenate(blocks, axis=1)
     placed[...] = jnp.dot(matrix, traces, precision=highest, preferred_element_type=f32)
 
@@ -378,18 +383,20 @@
         [jnp.broadcast_to(counts[:, b : b + 1].astype(f32), (1, 8)) for b in range(2)], axis=0
     )
     lists = jnp.concatenate([slots[t].astype(f32) for t in range(3)] + [used], axis=0)
-    s1[pl.ds(144, 8), :] = jnp.concatenate([lists, jnp.zeros((8, 120), f32)], axis=1)
+    s1[pl.ds(120, 8), :] = jnp.concatenate([lists, jnp.zeros((8, 120), f32)], axis=1)
 
 
 def rim_kernel(nat, s1, r1):
     rim_message(nat, position()[1], r1)
 
 
-def others_kernel(nat, q, s1, r1, s0, r0):
-    par = position()
-    rim_message(nat, 1 - par[1], r0)
-    pack_sector(q, 1 - par[0], s0)
-    s0[pl.ds(144, 8), :] = s1[pl.ds(144, 8), :]
+def others_kernel(q, s1, r1, s0):
+    pack_sector(q, 1 - position()[0], s0)
+    s0[pl.ds(120, 8), :] = s1[pl.ds(120, 8), :]
+
+
+def other_rim_kernel(nat, s0, r0):
+    rim_message(nat, 1 - position()[1], r0)
 
 
 def ahead_kernel(q, m, counts, slots, acc):
@@ -413,7 +420,7 @@
 def middle_kernel(inner, q, m, s0, s1, tables, ga0, ga1, part, matrix, r1, placed, back, ahead):
     par = position()
     choose_sectors(par, ga0, ga1, back, ahead)
-    matrix[...] = mortar_matrix(s1[pl.ds(144, 8), :], ahead[pl.ds(144, 8), :], tables[...])
+    matrix[...] = mortar_matrix(s1[pl.ds(120, 8), :], ahead[pl.ds(120, 8), :], tables[...])
     mortar = mortar_terms(par, matrix[...], s0, s1, back, ahead, placed)
     end_terms(q, m, inner, part, 1.0, range(5), sector_jumps(back, ahead, mortar), (2, 0))
     pack_blocks(part, m, par[1], r1)
@@ -453,7 +460,7 @@
 def sector_kernel(s, s1):
     par = position()
     pack_sector(s, par[0], s1)
-    s1[pl.ds(144, 8), :] = jnp.zeros((8, 128), f32)
+    s1[pl.ds(120, 8), :] = jnp.zeros((8, 128), f32)
 
 
 def later_kernel(s, part, m, s0, r0):
@@ -538,7 +545,7 @@
         gs0 = lax.ppermute(s0, "azim", az0)
         return gs0, gs1, gr0, gr1
 
-    state, rim, trace, first_trace = (2560, 128), (80, 128), (144, 128), (152, 128)
+    state, rim, trace, first_trace = (2560, 128), (80, 128), (120, 128), (128, 128)
     dma = pltpu.SemaphoreType.DMA
     turned = jnp.concatenate([projections[:2], projections[2:].transpose(0, 1, 3, 2)], axis=0)
     tables = jnp.repeat(turned.transpose(1, 0, 2, 3).reshape(16, 64), 8, axis=1)
@@ -551,11 +558,12 @@
     (early,) = call(ahead_kernel, [state])(q, m, counts, slots)
     (s1,) = call(first_kernel, [first_trace])(counts, q, slots, early)
     (r1,) = call(rim_kernel, [rim])(nat, s1)
-    s0, r0 = call(others_kernel, [first_trace, rim])(nat, q, s1, r1)
+    (s0,) = call(others_kernel, [first_trace])(q, s1, r1)
+    (r0,) = call(other_rim_kernel, [rim])(nat, s0)
     ga0, ga1, gr0, gr1 = across(r0, r1, s0, s1)
     (inner,) = call(inner_kernel, [state])(q, m, early)
     part, matrix, r1 = call(
-        middle_kernel, [state, (64, 128), (160, 128)], [(64, 256), first_trace, first_trace]
+        middle_kernel, [state, (64, 128), (136, 128)], [(64, 256), first_trace, first_trace]
     )(inner, q, m, s0, s1, tables, ga0, ga1)
     s, owed = call(block_kernel, [state, (1280, 128)], [rim, rim])(part, q, m, gr0, gr1)
     (s1,) = call(sector_kernel, [first_trace])(s)

time: 26.8 us -> 26.7 us (level)
    pallas_call x12 -> x13, Pallas kernels: 9.76 us -> 9.88 us  [run(): pl.pallas_call(kernel, out_shape=[jax.ShapeDtypeStruct(s, f32) for s in o...]
where the time goes in v3:
time: 26.7 us; the launch traced here: 26.6 us
  starting transfers between devices  12.9 us (48%)
  Pallas kernels  9.88 us (37%)
  waiting for transfers between devices  3.19 us (12%)
  between operations  0.33 us (1%)
  local copies, waits for them, and re-layouts  0.28 us (1%)
    pallas_call x13, Pallas kernels, run(): pl.pallas_call(kernel, out_shape=[jax.ShapeDtypeStruct(s, f32) for s in o...  9.88 us
    ppermute x2, starting transfers between devices, across(): gs1 = lax.ppermute(s1, 'azim', az1)  6.52 us
    ppermute x2, starting transfers between devices, across(): gr1 = lax.ppermute(r1, ('azim', 'radax'), rad1)  5.79 us
    ppermute x2, waiting for transfers between devices, across(): gr0 = lax.ppermute(r0, 'radax', rad0)  2.63 us
    ppermute x2, waiting for transfers between devices, across(): gs0 = lax.ppermute(s0, 'azim', az0)  0.55 us
  transfers between devices with their start and end apart: 8, of which 2 were waited for; matrix products, arithmetic and copies ran while one was open for 1% of the time, Pallas kernels for 16%

profile of v3, /device:TPU:16, one launch (start us, length us, event | category | flops | bytes accessed | tf_op | source)
XLA Modules:
  0.0 26.6 jit_solution(1688232597888671629)
XLA Ops:
  0.0 2.0 %shard_map.55 = (f32[8,128,320]{2,1,0:T(8,128)S(1)}, f32[2560,128]{1,0:T(8,128)S(1)}) custom-call(f32[8,128,320]{2,1,0:T(8,128)} %bitcast.18), custom_call_target="tpu_custom_call" | custom-call | bytes 3000000 | tf_op jit(solution)/shard_map/pallas_call | solution.py:509
  2.0 0.1 mul.13.m
  2.2 1.2 %shard_map.56.early.inner = f32[2560,128]{1,0:T(8,128)S(1)} custom-call(f32[2560,128]{1,0:T(8,128)S(1)} %get-tuple-element.14.q, f32[24,128]{1,0:T(8,128)S(1)} %mul.13.m, s32[1,2]{1,0:T(1,128)S(1)} %copy-done.1, s32[3,2,8]{2,1,0:T(2,128)S(1)} %bitcast.16), custom_call_target="tpu_custom_call" | custom-call | bytes 3000000 | tf_op jit(solution)/shard_map/pallas_call | solution.py:509
  3.3 0.2 shard_map.58.s1
  3.6 4.9 %collective-permute-start.1 = (f32[128,128]{1,0:T(8,128)S(1)}, f32[128,128]{1,0:T(8,128)S(1)}, u32[]{:S(2)}, u32[]{:S(2)}) collective-permute-start(f32[128,128]{1,0:T(8,128)S(1)} %shard_map.58.s1), channel_id=1, source_target_pairs={{0,248},{8,16},{16,8},{24,32},{32,24},{40,48},{48,40},{56,64},{64,... | collective-permute-start | bytes 196616 | tf_op jit(solution)/shard_map/ppermute | solution.py:543
  8.5 0.1 shard_map.59.r1
  8.6 0.0 copy-start.3
  8.6 2.9 %collective-permute-start.3 = (f32[80,128]{1,0:T(8,128)S(1)}, f32[80,128]{1,0:T(8,128)S(1)}, u32[]{:S(2)}, u32[]{:S(2)}) collective-permute-start(f32[80,128]{1,0:T(8,128)S(1)} %shard_map.59.r1), channel_id=1, source_target_pairs={{0,8},{1,2},{2,1},{3,4},{4,3},{5,6},{6,5},{7,15},{8,0},{9,10},{10,... | collective-permute-start | bytes 122888 | tf_op jit(solution)/shard_map/ppermute | solution.py:542
  11.5 0.2 shard_map.60.s0
  11.7 0.0 collective-permute-start
  11.7 0.1 shard_map.62
  11.9 0.2 collective-permute-start.2
  12.2 0.1 shard_map.57.inner
  12.3 0.1 copy.11
  12.4 0.5 %collective-permute-done.ga0 = f32[128,128]{1,0:T(8,128)S(1)} collective-permute-done((f32[128,128]{1,0:T(8,128)S(1)}, f32[128,128]{1,0:T(8,128)S(1)}, u32[]{:S(2)}, u32[]{:S(2)}) %collective-permute-start) | collective-permute-done | bytes 65568 | tf_op jit(solution)/shard_map/ppermute | solution.py:545
  13.0 0.0 collective-permute-done.1.ga1
  13.0 1.5 %shard_map.61 = (f32[2560,128]{1,0:T(8,128)S(1)}, f32[64,128]{1,0:T(8,128)S(1)}, f32[136,128]{1,0:T(8,128)S(1)}) custom-call(f32[2560,128]{1,0:T(8,128)S(1)} %shard_map.57.inner, f32[2560,128]{1,0:T(8,128)S(1)} %get-tuple-element.14.q, f32[24,128]{1,0:T(8,128)S(1)} %mul.13.m, f32[128,128]{1,0:T(8,128)S(1)} %shard_map.60.s0, f32[128,128]{1,0:T(8,128)S(1)} %shard_map.58.s1, ...), custom_call_target="tpu_custom_call" | custom-call | bytes 3000000 | tf_op jit(solution)/shard_map/pallas_call | solution.py:509
  14.5 2.9 %collective-permute-start.7 = (f32[136,128]{1,0:T(8,128)S(1)}, f32[136,128]{1,0:T(8,128)S(1)}, u32[]{:S(2)}, u32[]{:S(2)}) collective-permute-start(f32[136,128]{1,0:T(8,128)S(1)} %get-tuple-element.22), channel_id=1, source_target_pairs={{0,8},{1,2},{2,1},{3,4},{4,3},{5,6},{6,5},{7,15},{8,0},{9,10},{10,... | collective-permute-start | bytes 208904 | tf_op jit(solution)/shard_map/ppermute | solution.py:542
  17.3 0.0 collective-permute-done.2.gr0
  17.3 0.0 collective-permute-done.3.gr1
  17.3 0.3 %shard_map.63 = (f32[2560,128]{1,0:T(8,128)S(1)}, f32[1280,128]{1,0:T(8,128)S(1)}) custom-call(f32[2560,128]{1,0:T(8,128)S(1)} %get-tuple-element.16.part, f32[2560,128]{1,0:T(8,128)S(1)} %get-tuple-element.14.q, f32[24,128]{1,0:T(8,128)S(1)} %mul.13.m, f32[80,128]{1,0:T(8,128)S(1)} %collective-permute-done.2.gr0, f32[80,128]{1,0:T(8,128)S(1)} %collective-permute-done.3.gr1), custom_call_target="tpu_custom_call" | custom-call | bytes 3000000 | tf_op jit(solution)/shard_map/pallas_call | solution.py:509
  17.6 0.2 shard_map.66.s1
  17.9 1.6 %collective-permute-start.5 = (f32[128,128]{1,0:T(8,128)S(1)}, f32[128,128]{1,0:T(8,128)S(1)}, u32[]{:S(2)}, u32[]{:S(2)}) collective-permute-start(f32[128,128]{1,0:T(8,128)S(1)} %shard_map.66.s1), channel_id=1, source_target_pairs={{0,248},{8,16},{16,8},{24,32},{32,24},{40,48},{48,40},{56,64},{64,... | collective-permute-start | bytes 196616 | tf_op jit(solution)/shard_map/ppermute | solution.py:543
  19.5 0.4 %shard_map.65 = (f32[120,128]{1,0:T(8,128)S(1)}, f32[88,128]{1,0:T(8,128)S(1)}) custom-call(f32[2560,128]{1,0:T(8,128)S(1)} %get-tuple-element.17.s, f32[2560,128]{1,0:T(8,128)S(1)} %get-tuple-element.16.part, f32[24,128]{1,0:T(8,128)S(1)} %mul.13.m), custom_call_target="tpu_custom_call" | custom-call | bytes 3000000 | tf_op jit(solution)/shard_map/pallas_call | solution.py:509
  19.8 0.0 collective-permute-start.4
  19.9 0.3 %collective-permute-start.6 = (f32[88,128]{1,0:T(8,128)S(1)}, f32[88,128]{1,0:T(8,128)S(1)}, u32[]{:S(2)}, u32[]{:S(2)}) collective-permute-start(f32[88,128]{1,0:T(8,128)S(1)} %get-tuple-element.21), channel_id=1, source_target_pairs={{0,1},{1,0},{2,3},{3,2},{4,5},{5,4},{6,7},{7,6},{8,9},{9,8},{10,11... | collective-permute-start | bytes 135176 | tf_op jit(solution)/shard_map/ppermute | solution.py:544
  20.2 1.4 %shard_map.64.inner = f32[2560,128]{1,0:T(8,128)S(1)} custom-call(f32[2560,128]{1,0:T(8,128)S(1)} %get-tuple-element.17.s, f32[24,128]{1,0:T(8,128)S(1)} %mul.13.m, f32[2560,128]{1,0:T(8,128)S(1)} %get-tuple-element.14.q), custom_call_target="tpu_custom_call" | custom-call | bytes 3000000 | tf_op jit(solution)/shard_map/pallas_call | solution.py:509
  21.6 2.6 %collective-permute-done.6.gr0 = f32[88,128]{1,0:T(8,128)S(1)} collective-permute-done((f32[88,128]{1,0:T(8,128)S(1)}, f32[88,128]{1,0:T(8,128)S(1)}, u32[]{:S(2)}, u32[]{:S(2)}) %collective-permute-start.6) | collective-permute-done | bytes 45088 | tf_op jit(solution)/shard_map/ppermute | solution.py:544
  24.2 0.0 collective-permute-done.4.ga0
  24.2 0.0 collective-permute-done.5.ga1
  24.2 0.0 collective-permute-done.7.gr1
  24.2 2.2 %shard_map.67 = f32[8,128,320]{2,1,0:T(8,128)} custom-call(f32[2560,128]{1,0:T(8,128)S(1)} %shard_map.64.inner, f32[2560,128]{1,0:T(8,128)S(1)} %get-tuple-element.17.s, f32[24,128]{1,0:T(8,128)S(1)} %mul.13.m, f32[120,128]{1,0:T(8,128)S(1)} %get-tuple-element.18.s0, f32[128,128]{1,0:T(8,128)S(1)} %shard_map.66.s1, f32[64,128]{1,0:T(8,128)S(1)} %get-tuple-element.19.matrix, ...), custom_call_target="tpu_custom_call" | custom-call | bytes 3000000 | tf_op jit(solution)/shard_map/pallas_call | solution.py:509
  (15 shorter events, 0.1 us)
Async XLA Ops:
  0.0 2.0 %copy-start.2 = (f32[8,8,16,3]{2,1,3,0:T(8,128)S(1)}, f32[8,8,16,3]{2,1,3,0:T(8,128)}, u32[]{:S(2)}) copy-start(f32[8,8,16,3]{2,1,3,0:T(8,128)} %param.6) | copy-start | bytes 36868
  0.0 2.1 %copy-start = (s32[1,2,3,8]{3,1,2,0:T(2,128)S(1)}, s32[1,2,3,8]{3,1,2,0:T(2,128)}, u32[]{:S(2)}) copy-start(s32[1,2,3,8]{3,1,2,0:T(2,128)} %param.7) | copy-start | bytes 580
  0.0 2.1 %copy-start.1 = (s32[1,2]{1,0:T(1,128)S(1)}, s32[1,2]{1,0:T(1,128)}, u32[]{:S(2)}) copy-start(s32[1,2]{1,0:T(1,128)} %counts.3) | copy-start | bytes 28
  3.6 9.4 %collective-permute-start.1 = (f32[128,128]{1,0:T(8,128)S(1)}, f32[128,128]{1,0:T(8,128)S(1)}, u32[]{:S(2)}, u32[]{:S(2)}) collective-permute-start(f32[128,128]{1,0:T(8,128)S(1)} %shard_map.58.s1), channel_id=1, source_target_pairs={{0,248},{8,16},{16,8},{24,32},{32,24},{40,48},{48,40},{56,64},{64,... | collective-permute-start | bytes 196616 | tf_op jit(solution)/shard_map/ppermute | solution.py:543
  8.6 3.6 %copy-start.3 = (f32[4,16,4,4]{1,3,2,0:T(4,128)S(1)}, f32[4,16,4,4]{1,3,2,0:T(4,128)}, u32[]{:S(2)}) copy-start(f32[4,16,4,4]{1,3,2,0:T(4,128)} %param.9) | copy-start | bytes 12292
  8.6 8.8 %collective-permute-start.3 = (f32[80,128]{1,0:T(8,128)S(1)}, f32[80,128]{1,0:T(8,128)S(1)}, u32[]{:S(2)}, u32[]{:S(2)}) collective-permute-start(f32[80,128]{1,0:T(8,128)S(1)} %shard_map.59.r1), channel_id=1, source_target_pairs={{0,8},{1,2},{2,1},{3,4},{4,3},{5,6},{6,5},{7,15},{8,0},{9,10},{10,... | collective-permute-start | bytes 122888 | tf_op jit(solution)/shard_map/ppermute | solution.py:542
  11.7 1.3 %collective-permute-start = (f32[128,128]{1,0:T(8,128)S(1)}, f32[128,128]{1,0:T(8,128)S(1)}, u32[]{:S(2)}, u32[]{:S(2)}) collective-permute-start(f32[128,128]{1,0:T(8,128)S(1)} %shard_map.60.s0), channel_id=1, source_target_pairs={{0,8},{8,0},{16,24},{24,16},{32,40},{40,32},{48,56},{56,48},{64,72... | collective-permute-start | bytes 196616 | tf_op jit(solution)/shard_map/ppermute | solution.py:545
  11.9 5.5 %collective-permute-start.2 = (f32[80,128]{1,0:T(8,128)S(1)}, f32[80,128]{1,0:T(8,128)S(1)}, u32[]{:S(2)}, u32[]{:S(2)}) collective-permute-start(f32[80,128]{1,0:T(8,128)S(1)} %shard_map.62), channel_id=1, source_target_pairs={{0,1},{1,0},{2,3},{3,2},{4,5},{5,4},{6,7},{7,6},{8,9},{9,8},{10,11... | collective-permute-start | bytes 122888 | tf_op jit(solution)/shard_map/ppermute | solution.py:544
  14.5 9.8 %collective-permute-start.7 = (f32[136,128]{1,0:T(8,128)S(1)}, f32[136,128]{1,0:T(8,128)S(1)}, u32[]{:S(2)}, u32[]{:S(2)}) collective-permute-start(f32[136,128]{1,0:T(8,128)S(1)} %get-tuple-element.22), channel_id=1, source_target_pairs={{0,8},{1,2},{2,1},{3,4},{4,3},{5,6},{6,5},{7,15},{8,0},{9,10},{10,... | collective-permute-start | bytes 208904 | tf_op jit(solution)/shard_map/ppermute | solution.py:542
  17.9 6.4 %collective-permute-start.5 = (f32[128,128]{1,0:T(8,128)S(1)}, f32[128,128]{1,0:T(8,128)S(1)}, u32[]{:S(2)}, u32[]{:S(2)}) collective-permute-start(f32[128,128]{1,0:T(8,128)S(1)} %shard_map.66.s1), channel_id=1, source_target_pairs={{0,248},{8,16},{16,8},{24,32},{32,24},{40,48},{48,40},{56,64},{64,... | collective-permute-start | bytes 196616 | tf_op jit(solution)/shard_map/ppermute | solution.py:543
  19.8 4.4 %collective-permute-start.4 = (f32[120,128]{1,0:T(8,128)S(1)}, f32[120,128]{1,0:T(8,128)S(1)}, u32[]{:S(2)}, u32[]{:S(2)}) collective-permute-start(f32[120,128]{1,0:T(8,128)S(1)} %get-tuple-element.18.s0), channel_id=1, source_target_pairs={{0,8},{8,0},{16,24},{24,16},{32,40},{40,32},{48,56},{56,48},{64,72... | collective-permute-start | bytes 184328 | tf_op jit(solution)/shard_map/ppermute | solution.py:545
  19.9 4.3 %collective-permute-start.6 = (f32[88,128]{1,0:T(8,128)S(1)}, f32[88,128]{1,0:T(8,128)S(1)}, u32[]{:S(2)}, u32[]{:S(2)}) collective-permute-start(f32[88,128]{1,0:T(8,128)S(1)} %get-tuple-element.21), channel_id=1, source_target_pairs={{0,1},{1,0},{2,3},{3,2},{4,5},{5,4},{6,7},{7,6},{8,9},{9,8},{10,11... | collective-permute-start | bytes 135176 | tf_op jit(solution)/shard_map/ppermute | solution.py:544
